TPU v7x, 256 devices: a whole 4x4x8 slice. The times are simulated.
256 devices in a mesh: branch: 32 (over z, x), tensor: 8 (over y, core).
Axes of the slice: x: 4, y: 4, z: 8, core: 2. Of those that a mesh axis runs over, the one named last changes fastest.
Arguments:
- hidden: bfloat16 [4096, 4, 4096], P('branch', None, 'tensor'), may hold values from -6 to 6
- gain: float32 [4096], replicated, may hold values from 0.5 to 1.5
- w_query: bfloat16 [4096, 4096], P(None, 'tensor'), may hold values from -0.09375 to 0.09375
- w_keyval: bfloat16 [2, 4096, 1024], P(None, None, 'tensor'), may hold values from -0.09375 to 0.09375
- w_out: bfloat16 [4096, 4096], P('tensor'), may hold values from -0.09375 to 0.09375
- kv_codes: bfloat16 [1024, 2, 64, 1024], P('branch', None, None, 'tensor'), may hold values from -12 to 12
- kv_scales: bfloat16 [1024, 2, 8], P('branch', None, 'tensor'), may hold values from 0.5 to 24
- fork_export: int32 [256], P('branch'), may hold values from 0 to 31
- fork_pull: int32 [32, 64], replicated, may hold values from 0 to 255, as said below
- page_table: int32 [4096, 8], P('branch'), may hold values from 0 to 95
- lengths: int32 [4096], P('branch'), may hold values from 1 to 512, as said below
Outputs:
- mixed: bfloat16 [4096, 4, 4096], P('branch', None, 'tensor')
Inputs may be any that keep to these rules, and one draw needn't show every extreme that they name: `fork_pull`: an entry s * 8 + e names offered page e of group s. In each row at most 4 entries name one group, and some group is named exactly 4 times in every row. `lengths`: some branch has exactly 512 tokens.
All inputs are finite; a program needn't handle non-finite values.
Results may differ from a plain program's by a relative error of at most 0.017.
Values may be sent and summed in bfloat16 or wider, within the bound.
No kernel may reach another device: no remote copies, remote signals or barrier semaphores. Data moves between devices by JAX's collectives and lax.ppermute only.
A program may use at most 128 MiB of HBM per device.

v0:
```python
import functools
import math

import jax
import jax.numpy as jnp
from jax import lax
from jax.experimental import pallas as pl
from jax.experimental.pallas import tpu as pltpu
from jax.sharding import PartitionSpec as P

HEADS = 32
KVH = 8
HD = 128
PAGE = 64
MAXP = 8
STEPS = 4
GROUP = HEADS // KVH
OWN = 32
FORK = 64
EXPORT = 8
NZ, NX, NY = 8, 4, 4
ROWS = GROUP * STEPS
CODES = EXPORT * PAGE
PART = 2 * CODES + 16
TAKE = NZ * 4
FAR = NZ * PART
KPACK = TAKE * PAGE + 2 * TAKE
VPACK = TAKE * PAGE
KOWN = FAR + (NX - 1) * KPACK
VOWN = FAR + (NX - 1) * VPACK
SFAR = NZ * EXPORT
SOWN = SFAR + (NX - 1) * TAKE
BLOCK = 16
NEG = -1e30
LIMIT = 30 * 1024 * 1024


def from_z(value, d, name="z"):
    perm = [(z * NX + x, ((z - d) % NZ) * NX + x) for z in range(NZ) for x in range(NX)]
    with jax.named_scope(name):
        return lax.ppermute(value, "branch", perm)


def from_x(value, d, name="x"):
    perm = [(z * NX + x, z * NX + (x - d) % NX) for z in range(NZ) for x in range(NX)]
    with jax.named_scope(name):
        return lax.ppermute(value, "branch", perm)


def from_y(value, d, name="y"):
    perm = [(y * 2 + c, ((y - d) % NY) * 2 + c) for y in range(NY) for c in range(2)]
    with jax.named_scope(name):
        return lax.ppermute(value, "tensor", perm)


def from_core(value, name="core"):
    with jax.named_scope(name):
        return lax.ppermute(value, "tensor", [(t, t ^ 1) for t in range(2 * NY)])


def spec(space):
    return pl.BlockSpec(memory_space=space)


def export_kernel(picks, scales, codes, out, sems):
    copies = []
    for e in range(EXPORT):
        page = picks[e]
        for kind in range(2):
            rows = pl.ds(kind * CODES + e * PAGE, PAGE)
            copies.append(
                pltpu.make_async_copy(codes.at[page, kind], out.at[rows, :], sems.at[2 * e + kind])
            )
            copies[-1].start()
    place = lax.broadcasted_iota(jnp.int32, (16, HD), 0)
    rows = jnp.zeros((16, HD), jnp.float32)
    for e in range(EXPORT):
        for kind in range(2):
            rows = jnp.where(place == kind * EXPORT + e, scales[picks[e] * 2 + kind], rows)
    out[pl.ds(2 * CODES, 16), :] = rows.astype(jnp.bfloat16)
    for copy in copies:
        copy.wait()


def export_pages(codes, scales, picks):
    return pl.pallas_call(
        export_kernel,
        out_shape=jax.ShapeDtypeStruct((PART, HD), jnp.bfloat16),
        in_specs=[spec(pltpu.SMEM), spec(pltpu.SMEM), spec(pl.ANY)],
        out_specs=spec(pltpu.VMEM),
        scratch_shapes=[pltpu.SemaphoreType.DMA((2 * EXPORT,))],
        name="export_pages",
    )(picks, scales, codes)


def pack_kernel(kind, rows, marks, *refs):
    parts, outs = refs[:NZ], refs[NZ : NZ + NX - 1]
    pool, ksc, vsc, kout, vout, sems = refs[NZ + NX - 1 :]
    copies = load(parts, pool, sems)
    for copy in copies:
        copy.wait()
    for i in range(NZ):
        both = pool[pl.ds(i * PART + 2 * CODES, 16), :].astype(jnp.float32)
        ksc[pl.ds(i * EXPORT, EXPORT), :] = both[:EXPORT]
        vsc[pl.ds(i * EXPORT, EXPORT), :] = both[EXPORT:]
    for d, out in enumerate(outs):
        for k in range(TAKE):
            row = pl.multiple_of(rows[d * TAKE + k] + kind * CODES, 16)
            out[pl.ds(k * PAGE, PAGE), :] = pool[pl.ds(row, PAGE), :]
        if kind == 0:
            for k in range(TAKE):
                mark = marks[d * TAKE + k]
                kout[pl.ds(k, 1), :] = ksc[pl.ds(mark, 1), :]
                vout[pl.ds(k, 1), :] = vsc[pl.ds(mark, 1), :]
            out[pl.ds(TAKE * PAGE, TAKE), :] = kout[...].astype(jnp.bfloat16)
            out[pl.ds(TAKE * PAGE + TAKE, TAKE), :] = vout[...].astype(jnp.bfloat16)


def pack(kind, rows, marks, parts):
    out = jax.ShapeDtypeStruct((VPACK if kind else KPACK, HD), jnp.bfloat16)
    return pl.pallas_call(
        functools.partial(pack_kernel, kind),
        out_shape=(out,) * (NX - 1),
        in_specs=[spec(pltpu.SMEM)] * 2 + [spec(pl.ANY)] * NZ,
        out_specs=(spec(pltpu.VMEM),) * (NX - 1),
        scratch_shapes=[
            pltpu.VMEM((NZ * PART, HD), jnp.bfloat16),
            pltpu.VMEM((SFAR, HD), jnp.float32),
            pltpu.VMEM((SFAR, HD), jnp.float32),
            pltpu.VMEM((TAKE, HD), jnp.float32),
            pltpu.VMEM((TAKE, HD), jnp.float32),
            pltpu.SemaphoreType.DMA((NZ,)),
        ],
        name="pack",
    )(rows, marks, *parts)


def project_kernel(place, *refs):
    parts = refs[:8]
    gain, w_query, w_keyval, cosine, sine, q_out, k_out, v_out, qf = refs[8:]
    y, c = place[0], place[1]
    rows = parts[0].shape[0]
    width = parts[0].shape[1]
    power = jnp.zeros((rows, 1), jnp.float32)
    acc_q = jnp.zeros((rows, GROUP * HD), jnp.float32)
    acc_k = jnp.zeros((rows, HD), jnp.float32)
    acc_v = jnp.zeros((rows, HD), jnp.float32)
    for index, part in enumerate(parts):
        core = c if index < NY else 1 - c
        t = lax.rem(y + index % NY, NY) * 2 + core
        feats = part[...].astype(jnp.float32)
        power = power + jnp.sum(feats * feats, axis=1, keepdims=True)
        scaled = (feats * gain[pl.ds(t, 1), :]).astype(jnp.bfloat16)
        here = pl.ds(pl.multiple_of(t * width, width), width)
        acc_q = acc_q + jnp.dot(scaled, w_query[here, :], preferred_element_type=jnp.float32)
        acc_k = acc_k + jnp.dot(scaled, w_keyval[0, here, :], preferred_element_type=jnp.float32)
        acc_v = acc_v + jnp.dot(scaled, w_keyval[1, here, :], preferred_element_type=jnp.float32)
    norm = lax.rsqrt(power / (width * 8) + 1e-05)
    cos, sin = cosine[...], sine[...]

    def rope(v):
        return v * cos + pltpu.roll(v, HD // 2, 1) * sin

    for g in range(GROUP):
        head = rope(acc_q[:, g * HD : (g + 1) * HD] * norm) * HD ** (-0.5)
        qf[pl.ds(g, rows, stride=GROUP), :] = head
    q_out[...] = qf[...].astype(jnp.bfloat16)
    k_out[...] = rope(acc_k * norm).astype(jnp.bfloat16)
    v_out[...] = (acc_v * norm).astype(jnp.bfloat16)


def project(place, parts, gain, w_query, w_keyval, cosine, sine):
    rows = parts[0].shape[0]
    return pl.pallas_call(
        project_kernel,
        out_shape=(
            jax.ShapeDtypeStruct((rows * GROUP, HD), jnp.bfloat16),
            jax.ShapeDtypeStruct((rows, HD), jnp.bfloat16),
            jax.ShapeDtypeStruct((rows, HD), jnp.bfloat16),
        ),
        in_specs=[spec(pltpu.SMEM)] + [spec(pltpu.VMEM)] * 13,
        out_specs=(spec(pltpu.VMEM),) * 3,
        scratch_shapes=[pltpu.VMEM((rows * GROUP, HD), jnp.float32)],
        compiler_params=pltpu.CompilerParams(vmem_limit_bytes=LIMIT),
        name="project",
    )(place, *parts, gain, w_query, w_keyval, cosine, sine)


def load(parts, pool, sems):
    copies, at = [], 0
    for i, part in enumerate(parts):
        n = part.shape[0]
        copies.append(pltpu.make_async_copy(part, pool.at[pl.ds(at, n), :], sems.at[i]))
        copies[-1].start()
        at += n
    return copies


def pages(pool, where, slots):
    return jnp.concatenate(
        [pool[pl.ds(pl.multiple_of(where[s], 16), PAGE), :] for s in slots], axis=0
    )


def score_kernel(count, n, table, krow, mark, lens, q, k_new, v_new, own_scales, *refs):
    keys, refs = refs[:n], refs[n:]
    weights, fresh_out, pool, ksc, vsc, score, sems = refs
    copies = load(keys, pool, sems)
    for copy in copies:
        copy.wait()
    for part in range(NZ):
        both = pool[pl.ds(part * PART + 2 * CODES, 16), :].astype(jnp.float32)
        ksc[pl.ds(part * EXPORT, EXPORT), :] = both[:EXPORT]
        vsc[pl.ds(part * EXPORT, EXPORT), :] = both[EXPORT:]
    for part in range(NX - 1):
        at = FAR + part * KPACK + TAKE * PAGE
        ksc[pl.ds(SFAR + part * TAKE, TAKE), :] = pool[pl.ds(at, TAKE), :].astype(jnp.float32)
        vsc[pl.ds(SFAR + part * TAKE, TAKE), :] = pool[pl.ds(at + TAKE, TAKE), :].astype(
            jnp.float32
        )
    mine = own_scales[...].astype(jnp.float32)
    ksc[pl.ds(SOWN, OWN), :] = mine[:OWN]
    vsc[pl.ds(SOWN, OWN), :] = mine[OWN:]

    rows = BLOCK * ROWS
    span = 4 * PAGE
    lane = lax.broadcasted_iota(jnp.int32, (1, HD), 1)
    token = lax.broadcasted_iota(jnp.int32, (ROWS, span), 1)

    def scale_row(ref, slots):
        pieces = []
        for m in range(0, len(slots), 2):
            left = ref[pl.ds(mark[slots[m]], 1), :]
            right = ref[pl.ds(mark[slots[m + 1]], 1), :]
            pieces.append(jnp.where(lane < PAGE, left, right))
        return jnp.concatenate(pieces, axis=1)

    def one_block(block, carry):
        base = block * BLOCK
        here = pl.ds(pl.multiple_of(block * rows, rows), rows)
        queries = q[here, :]
        for i in range(BLOCK):
            branch = base + i
            length = lens[branch]
            for half in range(2):
                slots = [table[branch * MAXP + half * 4 + m] for m in range(4)]
                s = lax.dot_general(
                    queries[i * ROWS : (i + 1) * ROWS],
                    pages(pool, krow, slots),
                    (((1,), (1,)), ((), ())),
                    preferred_element_type=jnp.float32,
                )
                live = token < length - half * span
                score[pl.ds(i * ROWS, ROWS), pl.ds(half * span, span)] = jnp.where(
                    live, s * scale_row(ksc, slots), NEG
                )
        new = pl.ds(pl.multiple_of(base * STEPS, BLOCK * STEPS), BLOCK * STEPS)
        fresh = lax.dot_general(
            queries, k_new[new, :], (((1,), (1,)), ((), ())), preferred_element_type=jnp.float32
        )
        row = lax.broadcasted_iota(jnp.int32, fresh.shape, 0)
        col = lax.broadcasted_iota(jnp.int32, fresh.shape, 1)
        step = lax.shift_right_logical(row, 2)
        same = lax.shift_right_logical(step, 2) == lax.shift_right_logical(col, 2)
        fresh = jnp.where(same & ((step & 3) >= (col & 3)), fresh, NEG)
        context = score[...]
        top = jnp.maximum(
            jnp.max(context, axis=1, keepdims=True), jnp.max(fresh, axis=1, keepdims=True)
        )
        context = jnp.exp(context - top)
        fresh = jnp.exp(fresh - top)
        total = jnp.sum(context, axis=1, keepdims=True) + jnp.sum(fresh, axis=1, keepdims=True)
        inverse = 1.0 / total
        score[...] = context * inverse
        fresh_out[here, :] = jnp.dot(
            (fresh * inverse).astype(jnp.bfloat16),
            v_new[new, :],
            preferred_element_type=jnp.float32,
        )
        for i in range(BLOCK):
            branch = base + i
            slots = [table[branch * MAXP + m] for m in range(MAXP)]
            there = pl.ds(pl.multiple_of(block * rows + i * ROWS, ROWS), ROWS)
            weights[there, :] = (
                score[pl.ds(i * ROWS, ROWS), :] * scale_row(vsc, slots)
            ).astype(jnp.bfloat16)
        return carry

    lax.fori_loop(0, count // BLOCK, one_block, 0)


def score(table, krow, mark, lens, q, k_new, v_new, own_scales, keys):
    count = lens.shape[0]
    krows = sum(k.shape[0] for k in keys)
    return pl.pallas_call(
        functools.partial(score_kernel, count, len(keys)),
        out_shape=(
            jax.ShapeDtypeStruct((count * ROWS, MAXP * PAGE), jnp.bfloat16),
            jax.ShapeDtypeStruct((count * ROWS, HD), jnp.float32),
        ),
        in_specs=[spec(pltpu.SMEM)] * 4 + [spec(pltpu.VMEM)] * 4 + [spec(pl.ANY)] * len(keys),
        out_specs=(spec(pltpu.VMEM),) * 2,
        scratch_shapes=[
            pltpu.VMEM((krows, HD), jnp.bfloat16),
            pltpu.VMEM((SOWN + OWN, HD), jnp.float32),
            pltpu.VMEM((SOWN + OWN, HD), jnp.float32),
            pltpu.VMEM((BLOCK * ROWS, MAXP * PAGE), jnp.float32),
            pltpu.SemaphoreType.DMA((len(keys),)),
        ],
        compiler_params=pltpu.CompilerParams(vmem_limit_bytes=LIMIT),
        name="score",
    )(table, krow, mark, lens, q, k_new, v_new, own_scales, *keys)


def value_kernel(first, count, n, table, vrow, weights, fresh, *refs):
    values, (out, pool, result, sems) = refs[:n], refs[n:]
    copies = load(values, pool, sems)
    for copy in copies:
        copy.wait()

    def one_block(block, carry):
        for i in range(BLOCK):
            branch = first + block * BLOCK + i
            slots = [table[branch * MAXP + m] for m in range(MAXP)]
            here = pl.ds(pl.multiple_of((block * BLOCK + i) * ROWS, ROWS), ROWS)
            part = jnp.dot(
                weights[here, :], pages(pool, vrow, slots), preferred_element_type=jnp.float32
            )
            result[here, :] = part + fresh[here, :]
        return carry

    lax.fori_loop(0, count // BLOCK, one_block, 0)
    for g in range(GROUP):
        out[:, g * HD : (g + 1) * HD] = result[
            pl.ds(g, count * STEPS, stride=GROUP), :
        ].astype(jnp.bfloat16)


def value(first, count, table, vrow, weights, fresh, values):
    vrows = sum(v.shape[0] for v in values)
    chunk = first // count
    return pl.pallas_call(
        functools.partial(value_kernel, first, count, len(values)),
        grid=(1,),
        out_shape=jax.ShapeDtypeStruct((count * STEPS, GROUP * HD), jnp.bfloat16),
        in_specs=[spec(pltpu.SMEM)] * 2
        + [
            pl.BlockSpec((count * ROWS, MAXP * PAGE), lambda i: (chunk, 0)),
            pl.BlockSpec((count * ROWS, HD), lambda i: (chunk, 0)),
        ]
        + [spec(pl.ANY)] * len(values),
        out_specs=spec(pltpu.VMEM),
        scratch_shapes=[
            pltpu.VMEM((vrows, HD), jnp.bfloat16),
            pltpu.VMEM((count * ROWS, HD), jnp.float32),
            pltpu.SemaphoreType.DMA((len(values),)),
        ],
        compiler_params=pltpu.CompilerParams(vmem_limit_bytes=LIMIT),
        name="value",
    )(table, vrow, weights, fresh, *values)


def mix_kernel(place, near, far, w_near, w_far, *outs):
    y, c = place[0], place[1]
    width = outs[0].shape[1]
    for j in (2, 1, 3, 0):
        at = pl.ds(pl.multiple_of((lax.rem(y + j, NY) * 2 + c) * width, width), width)
        total = jnp.dot(near[...], w_near[:, at], preferred_element_type=jnp.float32)
        total += jnp.dot(far[...], w_far[:, at], preferred_element_type=jnp.float32)
        outs[j][...] = total.astype(jnp.bfloat16)


def mix(place, near, far, w_near, w_far):
    tokens = near.shape[0]
    width = w_near.shape[1] // (2 * NY)
    out = jax.ShapeDtypeStruct((tokens, width), jnp.bfloat16)
    return pl.pallas_call(
        mix_kernel,
        out_shape=(out,) * NY,
        in_specs=[spec(pltpu.SMEM)] + [spec(pltpu.VMEM)] * 4,
        out_specs=(spec(pltpu.VMEM),) * NY,
        compiler_params=pltpu.CompilerParams(vmem_limit_bytes=LIMIT),
        name="mix",
    )(place, near, far, w_near, w_far)


def after(value, *others):
    return lax.optimization_barrier((value, *others))[0]


def plan_kernel(where, pull, rows, marks, krow, vrow, mark):
    z, x = where[0], where[1]

    def locate(j, side):
        name = pull[(z * NX + lax.rem(x + side, NX)) * FORK + j]
        source = lax.shift_right_logical(name, 3)
        dz = lax.shift_right_logical(source, 2) - z
        dx = (source & (NX - 1)) - x
        return name & (EXPORT - 1), dz & (NZ - 1), dx & (NX - 1)

    def clear(k, carry):
        rows[k] = 0
        marks[k] = 0
        return carry

    lax.fori_loop(0, (NX - 1) * TAKE, clear, 0, unroll=8)
    for side in range(1, NX):

        def send(j, count):
            entry, dz, dx = locate(j, side)
            match = dx == 0
            at = jnp.where(match, (side - 1) * TAKE + count, (NX - 1) * TAKE)
            rows[at] = dz * PART + entry * PAGE
            marks[at] = dz * EXPORT + entry
            return count + match.astype(jnp.int32)

        lax.fori_loop(0, FORK, send, 0, unroll=8)

    def take(j, counts):
        entry, dz, dx = locate(j, 0)
        rank = jnp.where(dx == 1, counts[0], jnp.where(dx == 2, counts[1], counts[2]))
        near = dx == 0
        krow[j] = jnp.where(
            near, dz * PART + entry * PAGE, FAR + (dx - 1) * KPACK + rank * PAGE
        )
        mark[j] = jnp.where(near, dz * EXPORT + entry, SFAR + (dx - 1) * TAKE + rank)
        vrow[j] = jnp.where(
            near, dz * PART + CODES + entry * PAGE, FAR + (dx - 1) * VPACK + rank * PAGE
        )
        return tuple(counts[k] + (dx == k + 1).astype(jnp.int32) for k in range(NX - 1))

    zero = jnp.int32(0)
    lax.fori_loop(0, FORK, take, (zero,) * (NX - 1), unroll=8)

    def own(i, carry):
        krow[FORK + i] = KOWN + i * PAGE
        vrow[FORK + i] = VOWN + i * PAGE
        mark[FORK + i] = SOWN + i
        return carry

    lax.fori_loop(0, OWN, own, 0, unroll=8)


def plan(where, fork_pull):
    sends = jax.ShapeDtypeStruct(((NX - 1) * TAKE + 1,), jnp.int32)
    slots = jax.ShapeDtypeStruct((FORK + OWN,), jnp.int32)
    return pl.pallas_call(
        plan_kernel,
        out_shape=(sends, sends, slots, slots, slots),
        in_specs=[spec(pltpu.SMEM)] * 2,
        out_specs=(spec(pltpu.SMEM),) * 5,
        name="plan",
    )(where, fork_pull.reshape(-1))


def per_device(
    hidden,
    gain,
    w_query,
    w_keyval,
    w_out,
    kv_codes,
    kv_scales,
    fork_export,
    fork_pull,
    page_table,
    lengths,
):
    branches, steps, width = hidden.shape
    rows = branches * steps
    tensor = lax.axis_index("tensor")
    myself = lax.axis_index("branch")
    place = jnp.stack([tensor // 2, tensor % 2]).astype(jnp.int32)

    where = jnp.stack([myself // NX, myself % NX]).astype(jnp.int32)
    flat_scales = kv_scales.astype(jnp.float32).reshape(-1)
    part = export_pages(kv_codes, flat_scales, fork_export)
    own = after(hidden.reshape(rows, width), part)
    z = {0: part, 1: from_z(part, 1, "pages1"), -1: from_z(part, -1, "pages1")}
    aside = [from_y(own, d, "hidden") for d in (1, 2, 3)]
    w_far = from_core(w_out, "w_out")
    own_far = from_core(own, "hidden_core")
    z[2] = from_z(after(z[1], own_far, w_far), 1, "pages2")
    z[-2] = from_z(after(z[-1], own_far, w_far), -1, "pages2")
    where = after(where, z[1], z[-1])
    send_rows, send_marks, krow, vrow, mark = plan(where, fork_pull)
    z[2], z[-2] = after(z[2], send_rows), after(z[-2], send_rows)
    z[3], z[-3] = from_z(z[2], 1, "pages3"), from_z(z[-2], -1, "pages3")
    z[4] = from_z(after(z[3], z[-3]), 1, "pages4")
    parts = [own, *aside, own_far]
    parts += [from_core(after(part, z[2], z[-2]), "hidden_core") for part in aside]
    column = [z[d] for d in (0, 1, 2, 3, 4, -3, -2, -1)]
    column[0] = after(column[0], *parts)

    def sides(plus, across, minus, name):
        return [from_x(minus, 1, name), from_x(across, 2, name), from_x(plus, -1, name)]

    packed = pack(0, send_rows, send_marks, column)
    keys = column + sides(*packed, "key_side")

    half = HD // 2
    freq = jnp.exp(-(2.0 * jnp.arange(half).astype(jnp.float32) / HD) * math.log(500000.0))
    positions = (lengths[:, None] + jnp.arange(steps, dtype=jnp.int32)[None, :]).reshape(-1)
    angle = positions.astype(jnp.float32)[:, None] * freq[None, :]
    cos, sin = jnp.cos(angle), jnp.sin(angle)
    cosine = jnp.concatenate([cos, cos], axis=1)
    sine = jnp.concatenate([-sin, sin], axis=1)
    q, k_new, v_new = project(
        place, parts, gain.reshape(2 * NY, width), w_query, w_keyval, cosine, sine
    )

    keys = keys + [kv_codes[:, 0].reshape(OWN * PAGE, HD)]
    own_scales = jnp.broadcast_to(
        jnp.transpose(kv_scales, (1, 0, 2)).reshape(2 * OWN, 1), (2 * OWN, HD)
    )
    table = page_table.reshape(-1)

    column[0] = after(column[0], q)
    plus, across, minus = pack(1, send_rows, send_marks, column)
    values = column + sides(plus, across, minus, "value_side")
    values = values + [kv_codes[:, 1].reshape(OWN * PAGE, HD)]
    weights, fresh = score(table, krow, mark, lengths, q, k_new, v_new, own_scales, keys)
    attended = value(0, branches, table, vrow, weights, fresh, values)
    other = from_core(attended, "attended_core")
    total, plus, across, minus = mix(place, attended, other, w_out, w_far)
    got = [
        from_y(across, -2, "output"),
        from_y(plus, -1, "output"),
        from_y(minus, -3, "output"),
    ]
    total = total.astype(jnp.float32)
    for piece in got:
        total = total + piece.astype(jnp.float32)
    return total.astype(jnp.bfloat16).reshape(branches, steps, width)


def solution(mesh):
    return jax.shard_map(
        per_device,
        mesh=mesh,
        in_specs=(
            P("branch", None, "tensor"),
            P(),
            P(None, "tensor"),
            P(None, None, "tensor"),
            P("tensor", None),
            P("branch", None, None, "tensor"),
            P("branch", None, "tensor"),
            P("branch"),
            P(),
            P("branch", None),
            P("branch"),
        ),
        out_specs=P("branch", None, "tensor"),
        check_vma=False,
    )
```

profile of v0, /device:TPU:2, one launch (start us, length us, event | category | flops | bytes accessed | tf_op | source)
XLA Modules:
  0.0 151.1 jit_solution(8715431133778704865)
XLA Ops:
  2.5 2.4 %export_pages.1.refs_0_ = bf16[1040,128]{1,0:T(8,128)(2,1)} custom-call(s32[8]{0:T(128)} %picks.1, f32[64]{0:T(128)} %reshape.54.scales, bf16[32,2,64,128]{3,2,1,0:T(8,128)(2,1)} %codes.1), custom_call_target="tpu_custom_call" | custom-call | tf_op jit(solution)/shard_map/export_pages/pallas_call | solution.py:86
  5.6 5.9 %collective-permute-start = (bf16[1040,128]{1,0:T(8,128)(2,1)}, bf16[1040,128]{1,0:T(8,128)(2,1)S(1)}, u32[]{:S(2)}, u32[]{:S(2)}) collective-permute-start(bf16[1040,128]{1,0:T(8,128)(2,1)} %export_pages.1.refs_0_), channel_id=1, source_target_pairs={{0,224},{8,232},{16,240},{24,248},{32,0},{40,8},{48,16},{56,24},{6... | collective-permute-start | bytes 798728 | tf_op jit(solution)/shard_map/pages1/ppermute | solution.py:41
  11.4 3.0 %collective-permute-start.2 = (bf16[512,512]{1,0:T(8,128)(2,1)S(1)}, bf16[512,512]{1,0:T(8,128)(2,1)S(1)}, u32[]{:S(2)}, u32[]{:S(2)}) collective-permute-start(bf16[512,512]{1,0:T(8,128)(2,1)S(1)} %reshape.50.refs_0_), channel_id=1, source_target_pairs={{0,6},{1,7},{2,0},{3,1},{4,2},{5,3},{6,4},{7,5},{8,14},{9,15},{10,... | collective-permute-start | bytes 1572872 | tf_op jit(solution)/shard_map/hidden/ppermute | solution.py:53
  14.4 3.2 %collective-permute-done.refs_1_ = bf16[1040,128]{1,0:T(8,128)(2,1)S(1)} collective-permute-done((bf16[1040,128]{1,0:T(8,128)(2,1)}, bf16[1040,128]{1,0:T(8,128)(2,1)S(1)}, u32[]{:S(2)}, u32[]{:S(2)}) %collective-permute-start) | collective-permute-done | bytes 266272 | tf_op jit(solution)/shard_map/pages1/ppermute | solution.py:41
  17.6 3.2 %collective-permute-start.3 = (bf16[512,512]{1,0:T(8,128)(2,1)S(1)}, bf16[512,512]{1,0:T(8,128)(2,1)}, u32[]{:S(2)}, u32[]{:S(2)}) collective-permute-start(bf16[512,512]{1,0:T(8,128)(2,1)S(1)} %reshape.50.refs_0_), channel_id=1, source_target_pairs={{0,4},{1,5},{2,6},{3,7},{4,0},{5,1},{6,2},{7,3},{8,12},{9,13},{10,... | collective-permute-start | bytes 1572872 | tf_op jit(solution)/shard_map/hidden/ppermute | solution.py:53
  22.3 3.6 %collective-permute-start.7 = (bf16[1040,128]{1,0:T(8,128)(2,1)S(1)}, bf16[1040,128]{1,0:T(8,128)(2,1)S(1)}, u32[]{:S(2)}, u32[]{:S(2)}) collective-permute-start(bf16[1040,128]{1,0:T(8,128)(2,1)S(1)} %collective-permute-done.refs_1_), channel_id=1, source_target_pairs={{0,224},{8,232},{16,240},{24,248},{32,0},{40,8},{48,16},{56,24},{6... | collective-permute-start | bytes 798728 | tf_op jit(solution)/shard_map/pages2/ppermute | solution.py:41
  26.0 1.4 reshape.49.pull
  28.0 4.1 %plan.1 = (s32[97]{0:T(128)}, s32[97]{0:T(128)}, s32[96]{0:T(128)}, s32[96]{0:T(128)}, s32[96]{0:T(128)}) custom-call(s32[2]{0:T(128)} %pad_add_fusion.1.where, s32[2048]{0:T(1024)} %reshape.49.pull), custom_call_target="tpu_custom_call" | custom-call | tf_op jit(solution)/shard_map/plan/pallas_call | solution.py:447
  32.1 1.8 %collective-permute-done.8.refs_6_ = bf16[1040,128]{1,0:T(8,128)(2,1)S(1)} collective-permute-done((bf16[1040,128]{1,0:T(8,128)(2,1)S(1)}, bf16[1040,128]{1,0:T(8,128)(2,1)S(1)}, u32[]{:S(2)}, u32[]{:S(2)}) %collective-permute-start.8) | collective-permute-done | bytes 266272 | tf_op jit(solution)/shard_map/pages2/ppermute | solution.py:41
  33.9 1.5 collective-permute-start.12
  38.1 5.4 %collective-permute-done.4.refs_3_ = bf16[512,512]{1,0:T(8,128)(2,1)} collective-permute-done((bf16[512,512]{1,0:T(8,128)(2,1)S(1)}, bf16[512,512]{1,0:T(8,128)(2,1)}, u32[]{:S(2)}, u32[]{:S(2)}) %collective-permute-start.4) | collective-permute-done | bytes 524320 | tf_op jit(solution)/shard_map/hidden/ppermute | solution.py:53
  43.6 3.7 %collective-permute-start.14 = (bf16[1040,128]{1,0:T(8,128)(2,1)S(1)}, bf16[1040,128]{1,0:T(8,128)(2,1)S(1)}, u32[]{:S(2)}, u32[]{:S(2)}) collective-permute-start(bf16[1040,128]{1,0:T(8,128)(2,1)S(1)} %collective-permute-done.12.refs_3_), channel_id=1, source_target_pairs={{0,224},{8,232},{16,240},{24,248},{32,0},{40,8},{48,16},{56,24},{6... | collective-permute-start | bytes 798728 | tf_op jit(solution)/shard_map/pages4/ppermute | solution.py:41
  48.2 5.4 %collective-permute-done.14.refs_4_ = bf16[1040,128]{1,0:T(8,128)(2,1)S(1)} collective-permute-done((bf16[1040,128]{1,0:T(8,128)(2,1)S(1)}, bf16[1040,128]{1,0:T(8,128)(2,1)S(1)}, u32[]{:S(2)}, u32[]{:S(2)}) %collective-permute-start.14) | collective-permute-done | bytes 266272 | tf_op jit(solution)/shard_map/pages4/ppermute | solution.py:41
  54.3 3.5 %pack.2 = (bf16[2112,128]{1,0:T(8,128)(2,1)}, bf16[2112,128]{1,0:T(8,128)(2,1)}, bf16[2112,128]{1,0:T(8,128)(2,1)}) custom-call(s32[97]{0:T(128)} %get-tuple-element.43.rows, s32[97]{0:T(128)} %get-tuple-element.55.marks, bf16[1040,128]{1,0:T(8,128)(2,1)} %export_pages.1.refs_0_, bf16[1040,128]{1,0:T(8,128)(2,1)} %copy-done.1, bf16[1040,128]{1,0:T(8,128)(2,1)} %copy-done.5, ...), custom_call_target="tpu_custom_call" | custom-call | tf_op jit(solution)/shard_map/pack/pallas_call | solution.py:121
  59.9 2.5 %collective-permute-start.16 = (bf16[2112,128]{1,0:T(8,128)(2,1)}, bf16[2112,128]{1,0:T(8,128)(2,1)}, u32[]{:S(2)}, u32[]{:S(2)}) collective-permute-start(bf16[2112,128]{1,0:T(8,128)(2,1)} %get-tuple-element.57), channel_id=1, source_target_pairs={{0,16},{8,24},{16,0},{24,8},{32,48},{40,56},{48,32},{56,40},{64,80... | collective-permute-start | bytes 1622024 | tf_op jit(solution)/shard_map/key_side/ppermute | solution.py:47
  62.4 1.8 %collective-permute-start.17 = (bf16[2112,128]{1,0:T(8,128)(2,1)}, bf16[2112,128]{1,0:T(8,128)(2,1)}, u32[]{:S(2)}, u32[]{:S(2)}) collective-permute-start(bf16[2112,128]{1,0:T(8,128)(2,1)} %get-tuple-element.58), channel_id=1, source_target_pairs={{0,8},{8,16},{16,24},{24,0},{32,40},{40,48},{48,56},{56,32},{64,72... | collective-permute-start | bytes 1622024 | tf_op jit(solution)/shard_map/key_side/ppermute | solution.py:47
  64.3 2.2 %copy-done.16 = bf16[4096,512]{1,0:T(8,128)(2,1)S(1)} copy-done((bf16[4096,512]{1,0:T(8,128)(2,1)S(1)}, bf16[4096,512]{1,0:T(8,128)(2,1)}, u32[]{:S(2)}) %copy-start.16) | copy-done | bytes 4194328
  66.4 1.6 %copy-done.17 = bf16[2,4096,128]{2,1,0:T(8,128)(2,1)S(1)} copy-done((bf16[2,4096,128]{2,1,0:T(8,128)(2,1)S(1)}, bf16[2,4096,128]{2,1,0:T(8,128)(2,1)}, u32[]{:S(2)}) %copy-start.17) | copy-done | bytes 2097176
  70.1 6.4 %project.1 = (bf16[2048,128]{1,0:T(8,128)(2,1)S(1)}, bf16[512,128]{1,0:T(8,128)(2,1)S(1)}, bf16[512,128]{1,0:T(8,128)(2,1)S(1)}) custom-call(s32[2]{0:T(128)S(1)} %pad_add_fusion.place, bf16[512,512]{1,0:T(8,128)(2,1)S(1)} %reshape.50.refs_0_, bf16[512,512]{1,0:T(8,128)(2,1)S(1)} %copy-done.21, bf16[512,512]{1,0:T(8,128)(2,1)} %collective-permute-done.3.refs_2_, ...), custom_call_target="tpu_custom_call" | custom-call | tf_op jit(solution)/shard_map/project/pallas_call | solution.py:174
  77.4 3.7 %pack.3 = (bf16[2048,128]{1,0:T(8,128)(2,1)}, bf16[2048,128]{1,0:T(8,128)(2,1)}, bf16[2048,128]{1,0:T(8,128)(2,1)}) custom-call(s32[97]{0:T(128)} %get-tuple-element.43.rows, s32[97]{0:T(128)} %get-tuple-element.55.marks, bf16[1040,128]{1,0:T(8,128)(2,1)} %export_pages.1.refs_0_, bf16[1040,128]{1,0:T(8,128)(2,1)} %copy-done.1, bf16[1040,128]{1,0:T(8,128)(2,1)} %copy-done.5, ...), custom_call_target="tpu_custom_call" | custom-call | tf_op jit(solution)/shard_map/pack/pallas_call | solution.py:121
  82.7 2.5 %collective-permute-start.20 = (bf16[2048,128]{1,0:T(8,128)(2,1)}, bf16[2048,128]{1,0:T(8,128)(2,1)}, u32[]{:S(2)}, u32[]{:S(2)}) collective-permute-start(bf16[2048,128]{1,0:T(8,128)(2,1)} %get-tuple-element.64), channel_id=1, source_target_pairs={{0,8},{8,16},{16,24},{24,0},{32,40},{40,48},{48,56},{56,32},{64,72... | collective-permute-start | bytes 1572872 | tf_op jit(solution)/shard_map/value_side/ppermute | solution.py:47
  86.9 1.8 %collective-permute-done.17.refs_10_ = bf16[2112,128]{1,0:T(8,128)(2,1)} collective-permute-done((bf16[2112,128]{1,0:T(8,128)(2,1)}, bf16[2112,128]{1,0:T(8,128)(2,1)}, u32[]{:S(2)}, u32[]{:S(2)}) %collective-permute-start.17) | collective-permute-done | bytes 540704 | tf_op jit(solution)/shard_map/key_side/ppermute | solution.py:47
  89.9 10.8 %score.1 = (bf16[2048,512]{1,0:T(8,128)(2,1)S(1)}, f32[2048,128]{1,0:T(8,128)S(1)}) custom-call(s32[1024]{0:T(1024)S(1)} %reshape.46.table, s32[96]{0:T(128)S(1)} %copy-done.26, s32[96]{0:T(128)S(1)} %copy-done.27, s32[128]{0:T(128)S(1)} %copy-done.24, bf16[2048,128]{1,0:T(8,128)(2,1)S(1)} %copy-done.23, bf16[512,128]{1,0:T(8,128)(2,1)S(1)} %get-tuple-element.51.k_new, ...), custom_call_target="tpu_custom_call" | custom-call | tf_op jit(solution)/shard_map/score/pallas_call | solution.py:295
  100.7 6.6 %collective-permute-done.19.refs_9_ = bf16[2048,128]{1,0:T(8,128)(2,1)} collective-permute-done((bf16[2048,128]{1,0:T(8,128)(2,1)}, bf16[2048,128]{1,0:T(8,128)(2,1)}, u32[]{:S(2)}, u32[]{:S(2)}) %collective-permute-start.19) | collective-permute-done | bytes 524320 | tf_op jit(solution)/shard_map/value_side/ppermute | solution.py:47
  107.3 2.3 %collective-permute-done.20.refs_10_ = bf16[2048,128]{1,0:T(8,128)(2,1)} collective-permute-done((bf16[2048,128]{1,0:T(8,128)(2,1)}, bf16[2048,128]{1,0:T(8,128)(2,1)}, u32[]{:S(2)}, u32[]{:S(2)}) %collective-permute-start.20) | collective-permute-done | bytes 524320 | tf_op jit(solution)/shard_map/value_side/ppermute | solution.py:47
  109.6 5.4 %value.1.near = bf16[512,512]{1,0:T(8,128)(2,1)S(1)} custom-call(s32[1024]{0:T(1024)S(1)} %reshape.46.table, s32[96]{0:T(128)S(1)} %copy-done.25, bf16[2048,512]{1,0:T(8,128)(2,1)S(1)} %get-tuple-element.59.weights, f32[2048,128]{1,0:T(8,128)S(1)} %get-tuple-element.60.fresh, bf16[1040,128]{1,0:T(8,128)(2,1)S(1)} %copy-done, ...), custom_call_target="tpu_custom_call" | custom-call | tf_op jit(solution)/shard_map/value/pallas_call | solution.py:342
  115.3 1.9 %collective-permute-done.21.far = bf16[512,512]{1,0:T(8,128)(2,1)S(1)} collective-permute-done((bf16[512,512]{1,0:T(8,128)(2,1)S(1)}, bf16[512,512]{1,0:T(8,128)(2,1)S(1)}, u32[]{:S(2)}, u32[]{:S(2)}) %collective-permute-start.21) | collective-permute-done | bytes 524320 | tf_op jit(solution)/shard_map/attended_core/ppermute | solution.py:58
  117.2 4.5 %mix.1 = (bf16[512,512]{1,0:T(8,128)(2,1)S(1)}, bf16[512,512]{1,0:T(8,128)(2,1)S(1)}, bf16[512,512]{1,0:T(8,128)(2,1)S(1)}, bf16[512,512]{1,0:T(8,128)(2,1)S(1)}) custom-call(s32[2]{0:T(128)S(1)} %pad_add_fusion.place, bf16[512,512]{1,0:T(8,128)(2,1)S(1)} %value.1.near, bf16[512,512]{1,0:T(8,128)(2,1)S(1)} %collective-permute-done.21.far, ...), custom_call_target="tpu_custom_call" | custom-call | tf_op jit(solution)/shard_map/mix/pallas_call | solution.py:377
  122.4 1.4 collective-permute-start.23
  123.8 3.2 %collective-permute-start.22 = (bf16[512,512]{1,0:T(8,128)(2,1)S(1)}, bf16[512,512]{1,0:T(8,128)(2,1)S(1)}, u32[]{:S(2)}, u32[]{:S(2)}) collective-permute-start(bf16[512,512]{1,0:T(8,128)(2,1)S(1)} %get-tuple-element.66), channel_id=1, source_target_pairs={{0,4},{1,5},{2,6},{3,7},{4,0},{5,1},{6,2},{7,3},{8,12},{9,13},{10,... | collective-permute-start | bytes 1572872 | tf_op jit(solution)/shard_map/output/ppermute | solution.py:53
  127.0 9.5 %collective-permute-done.24 = bf16[512,512]{1,0:T(8,128)(2,1)S(1)} collective-permute-done((bf16[512,512]{1,0:T(8,128)(2,1)S(1)}, bf16[512,512]{1,0:T(8,128)(2,1)S(1)}, u32[]{:S(2)}, u32[]{:S(2)}) %collective-permute-start.24) | collective-permute-done | bytes 524320 | tf_op jit(solution)/shard_map/output/ppermute | solution.py:53
  137.5 12.4 %collective-permute-done.22 = bf16[512,512]{1,0:T(8,128)(2,1)S(1)} collective-permute-done((bf16[512,512]{1,0:T(8,128)(2,1)S(1)}, bf16[512,512]{1,0:T(8,128)(2,1)S(1)}, u32[]{:S(2)}, u32[]{:S(2)}) %collective-permute-start.22) | collective-permute-done | bytes 524320 | tf_op jit(solution)/shard_map/output/ppermute | solution.py:53
  (107 shorter events, 22.0 us)
Async XLA Ops:
  0.0 64.2 %copy-start.28 = (f32[4096]{0:T(1024)S(1)}, f32[4096]{0:T(1024)}, u32[]{:S(2)}) copy-start(f32[4096]{0:T(1024)} %param.12) | copy-start | bytes 49156
  0.0 22.3 %collective-permute-start.6 = (bf16[512,4096]{1,0:T(8,128)(2,1)}, bf16[512,4096]{1,0:T(8,128)(2,1)}, u32[]{:S(2)}, u32[]{:S(2)}) collective-permute-start(bf16[512,4096]{1,0:T(8,128)(2,1)} %w_near.1), channel_id=1, source_target_pairs={{0,1},{1,0},{2,3},{3,2},{4,5},{5,4},{6,7},{7,6},{8,9},{9,8},{10,11... | collective-permute-start | bytes 12582920 | tf_op jit(solution)/shard_map/w_out/ppermute | solution.py:58
  5.0 15.9 %collective-permute-start.5 = (bf16[512,512]{1,0:T(8,128)(2,1)S(1)}, bf16[512,512]{1,0:T(8,128)(2,1)S(1)}, u32[]{:S(2)}, u32[]{:S(2)}) collective-permute-start(bf16[512,512]{1,0:T(8,128)(2,1)S(1)} %reshape.50.refs_0_), channel_id=1, source_target_pairs={{0,1},{1,0},{2,3},{3,2},{4,5},{5,4},{6,7},{7,6},{8,9},{9,8},{10,11... | collective-permute-start | bytes 1572872 | tf_op jit(solution)/shard_map/hidden_core/ppermute | solution.py:58
  5.6 12.1 %collective-permute-start = (bf16[1040,128]{1,0:T(8,128)(2,1)}, bf16[1040,128]{1,0:T(8,128)(2,1)S(1)}, u32[]{:S(2)}, u32[]{:S(2)}) collective-permute-start(bf16[1040,128]{1,0:T(8,128)(2,1)} %export_pages.1.refs_0_), channel_id=1, source_target_pairs={{0,224},{8,232},{16,240},{24,248},{32,0},{40,8},{48,16},{56,24},{6... | collective-permute-start | bytes 798728 | tf_op jit(solution)/shard_map/pages1/ppermute | solution.py:41
  11.4 14.5 %collective-permute-start.1 = (bf16[1040,128]{1,0:T(8,128)(2,1)}, bf16[1040,128]{1,0:T(8,128)(2,1)S(1)}, u32[]{:S(2)}, u32[]{:S(2)}) collective-permute-start(bf16[1040,128]{1,0:T(8,128)(2,1)} %export_pages.1.refs_0_), channel_id=1, source_target_pairs={{0,32},{8,40},{16,48},{24,56},{32,64},{40,72},{48,80},{56,88},{64,... | collective-permute-start | bytes 798728 | tf_op jit(solution)/shard_map/pages1/ppermute | solution.py:41
  11.4 25.4 %collective-permute-start.2 = (bf16[512,512]{1,0:T(8,128)(2,1)S(1)}, bf16[512,512]{1,0:T(8,128)(2,1)S(1)}, u32[]{:S(2)}, u32[]{:S(2)}) collective-permute-start(bf16[512,512]{1,0:T(8,128)(2,1)S(1)} %reshape.50.refs_0_), channel_id=1, source_target_pairs={{0,6},{1,7},{2,0},{3,1},{4,2},{5,3},{6,4},{7,5},{8,14},{9,15},{10,... | collective-permute-start | bytes 1572872 | tf_op jit(solution)/shard_map/hidden/ppermute | solution.py:53
  17.6 35.9 %copy-start.1 = (bf16[1040,128]{1,0:T(8,128)(2,1)}, bf16[1040,128]{1,0:T(8,128)(2,1)S(1)}, u32[]{:S(2)}) copy-start(bf16[1040,128]{1,0:T(8,128)(2,1)S(1)} %collective-permute-done.refs_1_) | copy-start | bytes 798724
  17.6 20.0 %collective-permute-start.3 = (bf16[512,512]{1,0:T(8,128)(2,1)S(1)}, bf16[512,512]{1,0:T(8,128)(2,1)}, u32[]{:S(2)}, u32[]{:S(2)}) collective-permute-start(bf16[512,512]{1,0:T(8,128)(2,1)S(1)} %reshape.50.refs_0_), channel_id=1, source_target_pairs={{0,4},{1,5},{2,6},{3,7},{4,0},{5,1},{6,2},{7,3},{8,12},{9,13},{10,... | collective-permute-start | bytes 1572872 | tf_op jit(solution)/shard_map/hidden/ppermute | solution.py:53
  21.7 21.9 %collective-permute-start.4 = (bf16[512,512]{1,0:T(8,128)(2,1)S(1)}, bf16[512,512]{1,0:T(8,128)(2,1)}, u32[]{:S(2)}, u32[]{:S(2)}) collective-permute-start(bf16[512,512]{1,0:T(8,128)(2,1)S(1)} %reshape.50.refs_0_), channel_id=1, source_target_pairs={{0,2},{1,3},{2,4},{3,5},{4,6},{5,7},{6,0},{7,1},{8,10},{9,11},{10,... | collective-permute-start | bytes 1572872 | tf_op jit(solution)/shard_map/hidden/ppermute | solution.py:53
  22.3 9.7 %collective-permute-start.7 = (bf16[1040,128]{1,0:T(8,128)(2,1)S(1)}, bf16[1040,128]{1,0:T(8,128)(2,1)S(1)}, u32[]{:S(2)}, u32[]{:S(2)}) collective-permute-start(bf16[1040,128]{1,0:T(8,128)(2,1)S(1)} %collective-permute-done.refs_1_), channel_id=1, source_target_pairs={{0,224},{8,232},{16,240},{24,248},{32,0},{40,8},{48,16},{56,24},{6... | collective-permute-start | bytes 798728 | tf_op jit(solution)/shard_map/pages2/ppermute | solution.py:41
  25.9 27.6 %copy-start.3 = (bf16[1040,128]{1,0:T(8,128)(2,1)}, bf16[1040,128]{1,0:T(8,128)(2,1)S(1)}, u32[]{:S(2)}) copy-start(bf16[1040,128]{1,0:T(8,128)(2,1)S(1)} %collective-permute-done.1.refs_7_) | copy-start | bytes 798724
  25.9 7.9 %collective-permute-start.8 = (bf16[1040,128]{1,0:T(8,128)(2,1)S(1)}, bf16[1040,128]{1,0:T(8,128)(2,1)S(1)}, u32[]{:S(2)}, u32[]{:S(2)}) collective-permute-start(bf16[1040,128]{1,0:T(8,128)(2,1)S(1)} %collective-permute-done.1.refs_7_), channel_id=1, source_target_pairs={{0,32},{8,40},{16,48},{24,56},{32,64},{40,72},{48,80},{56,88},{64,... | collective-permute-start | bytes 798728 | tf_op jit(solution)/shard_map/pages2/ppermute | solution.py:41
  32.1 21.5 %copy-start.5 = (bf16[1040,128]{1,0:T(8,128)(2,1)}, bf16[1040,128]{1,0:T(8,128)(2,1)S(1)}, u32[]{:S(2)}) copy-start(bf16[1040,128]{1,0:T(8,128)(2,1)S(1)} %collective-permute-done.7.refs_2_) | copy-start | bytes 798724
  33.9 19.7 %copy-start.7 = (bf16[1040,128]{1,0:T(8,128)(2,1)}, bf16[1040,128]{1,0:T(8,128)(2,1)S(1)}, u32[]{:S(2)}) copy-start(bf16[1040,128]{1,0:T(8,128)(2,1)S(1)} %collective-permute-done.8.refs_6_) | copy-start | bytes 798724
  33.9 9.7 %collective-permute-start.12 = (bf16[1040,128]{1,0:T(8,128)(2,1)S(1)}, bf16[1040,128]{1,0:T(8,128)(2,1)S(1)}, u32[]{:S(2)}, u32[]{:S(2)}) collective-permute-start(bf16[1040,128]{1,0:T(8,128)(2,1)S(1)} %collective-permute-done.7.refs_2_), channel_id=1, source_target_pairs={{0,224},{8,232},{16,240},{24,248},{32,0},{40,8},{48,16},{56,24},{6... | collective-permute-start | bytes 798728 | tf_op jit(solution)/shard_map/pages3/ppermute | solution.py:41
  35.4 8.2 %collective-permute-start.13 = (bf16[1040,128]{1,0:T(8,128)(2,1)S(1)}, bf16[1040,128]{1,0:T(8,128)(2,1)S(1)}, u32[]{:S(2)}, u32[]{:S(2)}) collective-permute-start(bf16[1040,128]{1,0:T(8,128)(2,1)S(1)} %collective-permute-done.8.refs_6_), channel_id=1, source_target_pairs={{0,32},{8,40},{16,48},{24,56},{32,64},{40,72},{48,80},{56,88},{64,... | collective-permute-start | bytes 798728 | tf_op jit(solution)/shard_map/pages3/ppermute | solution.py:41
  36.8 11.3 %collective-permute-start.9 = (bf16[512,512]{1,0:T(8,128)(2,1)S(1)}, bf16[512,512]{1,0:T(8,128)(2,1)}, u32[]{:S(2)}, u32[]{:S(2)}) collective-permute-start(bf16[512,512]{1,0:T(8,128)(2,1)S(1)} %collective-permute-done.2.refs_1_), channel_id=1, source_target_pairs={{0,1},{1,0},{2,3},{3,2},{4,5},{5,4},{6,7},{7,6},{8,9},{9,8},{10,11... | collective-permute-start | bytes 1572872 | tf_op jit(solution)/shard_map/hidden_core/ppermute | solution.py:58
  37.6 10.5 %collective-permute-start.10 = (bf16[512,512]{1,0:T(8,128)(2,1)}, bf16[512,512]{1,0:T(8,128)(2,1)}, u32[]{:S(2)}, u32[]{:S(2)}) collective-permute-start(bf16[512,512]{1,0:T(8,128)(2,1)} %collective-permute-done.3.refs_2_), channel_id=1, source_target_pairs={{0,1},{1,0},{2,3},{3,2},{4,5},{5,4},{6,7},{7,6},{8,9},{9,8},{10,11... | collective-permute-start | bytes 1572872 | tf_op jit(solution)/shard_map/hidden_core/ppermute | solution.py:58
  43.6 4.6 %collective-permute-start.11 = (bf16[512,512]{1,0:T(8,128)(2,1)}, bf16[512,512]{1,0:T(8,128)(2,1)}, u32[]{:S(2)}, u32[]{:S(2)}) collective-permute-start(bf16[512,512]{1,0:T(8,128)(2,1)} %collective-permute-done.4.refs_3_), channel_id=1, source_target_pairs={{0,1},{1,0},{2,3},{3,2},{4,5},{5,4},{6,7},{7,6},{8,9},{9,8},{10,11... | collective-permute-start | bytes 1572872 | tf_op jit(solution)/shard_map/hidden_core/ppermute | solution.py:58
  43.6 10.0 %collective-permute-start.14 = (bf16[1040,128]{1,0:T(8,128)(2,1)S(1)}, bf16[1040,128]{1,0:T(8,128)(2,1)S(1)}, u32[]{:S(2)}, u32[]{:S(2)}) collective-permute-start(bf16[1040,128]{1,0:T(8,128)(2,1)S(1)} %collective-permute-done.12.refs_3_), channel_id=1, source_target_pairs={{0,224},{8,232},{16,240},{24,248},{32,0},{40,8},{48,16},{56,24},{6... | collective-permute-start | bytes 798728 | tf_op jit(solution)/shard_map/pages4/ppermute | solution.py:41
  57.8 24.9 %collective-permute-start.15 = (bf16[2112,128]{1,0:T(8,128)(2,1)}, bf16[2112,128]{1,0:T(8,128)(2,1)S(1)}, u32[]{:S(2)}, u32[]{:S(2)}) collective-permute-start(bf16[2112,128]{1,0:T(8,128)(2,1)} %get-tuple-element.56), channel_id=1, source_target_pairs={{0,24},{8,0},{16,8},{24,16},{32,56},{40,32},{48,40},{56,48},{64,88... | collective-permute-start | bytes 1622024 | tf_op jit(solution)/shard_map/key_side/ppermute | solution.py:47
  59.9 27.0 %collective-permute-start.16 = (bf16[2112,128]{1,0:T(8,128)(2,1)}, bf16[2112,128]{1,0:T(8,128)(2,1)}, u32[]{:S(2)}, u32[]{:S(2)}) collective-permute-start(bf16[2112,128]{1,0:T(8,128)(2,1)} %get-tuple-element.57), channel_id=1, source_target_pairs={{0,16},{8,24},{16,0},{24,8},{32,48},{40,56},{48,32},{56,40},{64,80... | collective-permute-start | bytes 1622024 | tf_op jit(solution)/shard_map/key_side/ppermute | solution.py:47
  62.4 26.3 %collective-permute-start.17 = (bf16[2112,128]{1,0:T(8,128)(2,1)}, bf16[2112,128]{1,0:T(8,128)(2,1)}, u32[]{:S(2)}, u32[]{:S(2)}) collective-permute-start(bf16[2112,128]{1,0:T(8,128)(2,1)} %get-tuple-element.58), channel_id=1, source_target_pairs={{0,8},{8,16},{16,24},{24,0},{32,40},{40,48},{48,56},{56,32},{64,72... | collective-permute-start | bytes 1622024 | tf_op jit(solution)/shard_map/key_side/ppermute | solution.py:47
  81.1 28.4 %copy-start.25 = (s32[96]{0:T(128)S(1)}, s32[96]{0:T(128)}, u32[]{:S(2)}) copy-start(s32[96]{0:T(128)} %get-tuple-element.38.vrow) | copy-start | bytes 1156
  81.2 19.5 %collective-permute-start.18 = (bf16[2048,128]{1,0:T(8,128)(2,1)}, bf16[2048,128]{1,0:T(8,128)(2,1)S(1)}, u32[]{:S(2)}, u32[]{:S(2)}) collective-permute-start(bf16[2048,128]{1,0:T(8,128)(2,1)} %get-tuple-element.62), channel_id=1, source_target_pairs={{0,24},{8,0},{16,8},{24,16},{32,56},{40,32},{48,40},{56,48},{64,88... | collective-permute-start | bytes 1572872 | tf_op jit(solution)/shard_map/value_side/ppermute | solution.py:47
  81.5 25.8 %collective-permute-start.19 = (bf16[2048,128]{1,0:T(8,128)(2,1)}, bf16[2048,128]{1,0:T(8,128)(2,1)}, u32[]{:S(2)}, u32[]{:S(2)}) collective-permute-start(bf16[2048,128]{1,0:T(8,128)(2,1)} %get-tuple-element.63), channel_id=1, source_target_pairs={{0,16},{8,24},{16,0},{24,8},{32,48},{40,56},{48,32},{56,40},{64,80... | collective-permute-start | bytes 1572872 | tf_op jit(solution)/shard_map/value_side/ppermute | solution.py:47
  82.7 26.8 %collective-permute-start.20 = (bf16[2048,128]{1,0:T(8,128)(2,1)}, bf16[2048,128]{1,0:T(8,128)(2,1)}, u32[]{:S(2)}, u32[]{:S(2)}) collective-permute-start(bf16[2048,128]{1,0:T(8,128)(2,1)} %get-tuple-element.64), channel_id=1, source_target_pairs={{0,8},{8,16},{16,24},{24,0},{32,40},{40,48},{48,56},{56,32},{64,72... | collective-permute-start | bytes 1572872 | tf_op jit(solution)/shard_map/value_side/ppermute | solution.py:47
  100.7 16.5 %copy-start.15 = (bf16[512,4096]{1,0:T(8,128)(2,1)S(1)}, bf16[512,4096]{1,0:T(8,128)(2,1)}, u32[]{:S(2)}) copy-start(bf16[512,4096]{1,0:T(8,128)(2,1)} %w_near.1) | copy-start | bytes 12582916
  115.0 2.2 %collective-permute-start.21 = (bf16[512,512]{1,0:T(8,128)(2,1)S(1)}, bf16[512,512]{1,0:T(8,128)(2,1)S(1)}, u32[]{:S(2)}, u32[]{:S(2)}) collective-permute-start(bf16[512,512]{1,0:T(8,128)(2,1)S(1)} %value.1.near), channel_id=1, source_target_pairs={{0,1},{1,0},{2,3},{3,2},{4,5},{5,4},{6,7},{7,6},{8,9},{9,8},{10,11... | collective-permute-start | bytes 1572872 | tf_op jit(solution)/shard_map/attended_core/ppermute | solution.py:58
  121.7 14.8 %collective-permute-start.24 = (bf16[512,512]{1,0:T(8,128)(2,1)S(1)}, bf16[512,512]{1,0:T(8,128)(2,1)S(1)}, u32[]{:S(2)}, u32[]{:S(2)}) collective-permute-start(bf16[512,512]{1,0:T(8,128)(2,1)S(1)} %get-tuple-element.68), channel_id=1, source_target_pairs={{0,6},{1,7},{2,0},{3,1},{4,2},{5,3},{6,4},{7,5},{8,14},{9,15},{10,... | collective-permute-start | bytes 1572872 | tf_op jit(solution)/shard_map/output/ppermute | solution.py:53
  122.4 15.1 %collective-permute-start.23 = (bf16[512,512]{1,0:T(8,128)(2,1)S(1)}, bf16[512,512]{1,0:T(8,128)(2,1)S(1)}, u32[]{:S(2)}, u32[]{:S(2)}) collective-permute-start(bf16[512,512]{1,0:T(8,128)(2,1)S(1)} %get-tuple-element.67), channel_id=1, source_target_pairs={{0,2},{1,3},{2,4},{3,5},{4,6},{5,7},{6,0},{7,1},{8,10},{9,11},{10,... | collective-permute-start | bytes 1572872 | tf_op jit(solution)/shard_map/output/ppermute | solution.py:53
  123.8 26.1 %collective-permute-start.22 = (bf16[512,512]{1,0:T(8,128)(2,1)S(1)}, bf16[512,512]{1,0:T(8,128)(2,1)S(1)}, u32[]{:S(2)}, u32[]{:S(2)}) collective-permute-start(bf16[512,512]{1,0:T(8,128)(2,1)S(1)} %get-tuple-element.66), channel_id=1, source_target_pairs={{0,4},{1,5},{2,6},{3,7},{4,0},{5,1},{6,2},{7,3},{8,12},{9,13},{10,... | collective-permute-start | bytes 1572872 | tf_op jit(solution)/shard_map/output/ppermute | solution.py:53
  (24 other events, 185.6 us)
where the time goes:
time: 154 us; the launch traced here: 151 us
  waiting for transfers between devices  52.2 us (34%)
  Pallas kernels  40.9 us (27%)
  starting transfers between devices  38 us (25%)
  local copies, waits for them, and re-layouts  16.7 us (11%)
  other arithmetic  2.89 us (2%)
    ppermute x6, waiting for transfers between devices, from_y(): return lax.ppermute(value, 'tensor', perm)  29.3 us
    ppermute x7, starting transfers between devices, from_z(): return lax.ppermute(value, 'branch', perm)  15.1 us
    ppermute x6, starting transfers between devices, from_y(): return lax.ppermute(value, 'tensor', perm)  12.2 us
    pallas_call x1, Pallas kernels, score(): pl.pallas_call(functools.partial(score_kernel, count, len(keys)), out_sha...  10.8 us
    ppermute x6, waiting for transfers between devices, from_x(): return lax.ppermute(value, 'branch', perm)  10.6 us
    ppermute x7, waiting for transfers between devices, from_z(): return lax.ppermute(value, 'branch', perm)  10.4 us
    unnamed x63, local copies, waits for them, and re-layouts  10.2 us
    ppermute x6, starting transfers between devices, from_x(): return lax.ppermute(value, 'branch', perm)  9.21 us
  transfers between devices with their start and end apart: 25, of which 12 were waited for; matrix products, arithmetic and copies ran while one was open for 5% of the time, Pallas kernels for 18%

commit v1 on v0

--- a/solution.py
+++ b/solution.py
@@ -74,9 +74,12 @@
             copies[-1].start()
     place = lax.broadcasted_iota(jnp.int32, (16, HD), 0)
     rows = jnp.zeros((16, HD), jnp.float32)
+    table = scales[...].astype(jnp.float32)
+    lane = lax.broadcasted_iota(jnp.int32, table.shape, 1)
     for e in range(EXPORT):
+        pair = jnp.sum(jnp.where(lane == picks[e], table, 0.0), axis=1, keepdims=True)
         for kind in range(2):
-            rows = jnp.where(place == kind * EXPORT + e, scales[picks[e] * 2 + kind], rows)
+            rows = jnp.where(place == kind * EXPORT + e, pair[kind : kind + 1, :], rows)
     out[pl.ds(2 * CODES, 16), :] = rows.astype(jnp.bfloat16)
     for copy in copies:
         copy.wait()
@@ -86,7 +89,7 @@
     return pl.pallas_call(
         export_kernel,
         out_shape=jax.ShapeDtypeStruct((PART, HD), jnp.bfloat16),
-        in_specs=[spec(pltpu.SMEM), spec(pltpu.SMEM), spec(pl.ANY)],
+        in_specs=[spec(pltpu.SMEM), spec(pltpu.VMEM), spec(pl.ANY)],
         out_specs=spec(pltpu.VMEM),
         scratch_shapes=[pltpu.SemaphoreType.DMA((2 * EXPORT,))],
         name="export_pages",
@@ -95,17 +98,25 @@
 
 def pack_kernel(kind, rows, marks, *refs):
     parts, outs = refs[:NZ], refs[NZ : NZ + NX - 1]
-    pool, ksc, vsc, kout, vout, sems = refs[NZ + NX - 1 :]
-    copies = load(parts, pool, sems)
+    pool, both, ksc, vsc, kout, vout, sems = refs[NZ + NX - 1 :]
+    copies = []
+    for i, part in enumerate(parts):
+        ends = ((part, kind * CODES, pool, CODES), (part, 2 * CODES, both, 16))
+        for source, at, target, n in ends[: 2 - kind]:
+            to = target.at[pl.ds(i * n, n), :]
+            sem = sems.at[2 * i + (target is both)]
+            copies.append(pltpu.make_async_copy(source.at[pl.ds(at, n), :], to, sem))
+            copies[-1].start()
     for copy in copies:
         copy.wait()
-    for i in range(NZ):
-        both = pool[pl.ds(i * PART + 2 * CODES, 16), :].astype(jnp.float32)
-        ksc[pl.ds(i * EXPORT, EXPORT), :] = both[:EXPORT]
-        vsc[pl.ds(i * EXPORT, EXPORT), :] = both[EXPORT:]
+    if kind == 0:
+        for i in range(NZ):
+            pair = both[pl.ds(i * 16, 16), :].astype(jnp.float32)
+            ksc[pl.ds(i * EXPORT, EXPORT), :] = pair[:EXPORT]
+            vsc[pl.ds(i * EXPORT, EXPORT), :] = pair[EXPORT:]
     for d, out in enumerate(outs):
         for k in range(TAKE):
-            row = pl.multiple_of(rows[d * TAKE + k] + kind * CODES, 16)
+            row = pl.multiple_of(rows[d * TAKE + k], 16)
             out[pl.ds(k * PAGE, PAGE), :] = pool[pl.ds(row, PAGE), :]
         if kind == 0:
             for k in range(TAKE):
@@ -124,12 +135,13 @@
         in_specs=[spec(pltpu.SMEM)] * 2 + [spec(pl.ANY)] * NZ,
         out_specs=(spec(pltpu.VMEM),) * (NX - 1),
         scratch_shapes=[
-            pltpu.VMEM((NZ * PART, HD), jnp.bfloat16),
+            pltpu.VMEM((NZ * CODES, HD), jnp.bfloat16),
+            pltpu.VMEM((NZ * 16, HD), jnp.bfloat16),
             pltpu.VMEM((SFAR, HD), jnp.float32),
             pltpu.VMEM((SFAR, HD), jnp.float32),
             pltpu.VMEM((TAKE, HD), jnp.float32),
             pltpu.VMEM((TAKE, HD), jnp.float32),
-            pltpu.SemaphoreType.DMA((NZ,)),
+            pltpu.SemaphoreType.DMA((2 * NZ,)),
         ],
         name="pack",
     )(rows, marks, *parts)
@@ -360,25 +372,25 @@
     )(table, vrow, weights, fresh, *values)
 
 
-def mix_kernel(place, near, far, w_near, w_far, *outs):
+def mix_kernel(blocks, place, near, far, w_near, w_far, *outs):
     y, c = place[0], place[1]
     width = outs[0].shape[1]
-    for j in (2, 1, 3, 0):
+    for j, out in zip(blocks, outs):
         at = pl.ds(pl.multiple_of((lax.rem(y + j, NY) * 2 + c) * width, width), width)
         total = jnp.dot(near[...], w_near[:, at], preferred_element_type=jnp.float32)
         total += jnp.dot(far[...], w_far[:, at], preferred_element_type=jnp.float32)
-        outs[j][...] = total.astype(jnp.bfloat16)
-
-
-def mix(place, near, far, w_near, w_far):
+        out[...] = total.astype(jnp.bfloat16)
+
+
+def mix(blocks, place, near, far, w_near, w_far):
     tokens = near.shape[0]
     width = w_near.shape[1] // (2 * NY)
     out = jax.ShapeDtypeStruct((tokens, width), jnp.bfloat16)
     return pl.pallas_call(
-        mix_kernel,
-        out_shape=(out,) * NY,
+        functools.partial(mix_kernel, blocks),
+        out_shape=(out,) * len(blocks),
         in_specs=[spec(pltpu.SMEM)] + [spec(pltpu.VMEM)] * 4,
-        out_specs=(spec(pltpu.VMEM),) * NY,
+        out_specs=(spec(pltpu.VMEM),) * len(blocks),
         compiler_params=pltpu.CompilerParams(vmem_limit_bytes=LIMIT),
         name="mix",
     )(place, near, far, w_near, w_far)
@@ -410,7 +422,7 @@
             entry, dz, dx = locate(j, side)
             match = dx == 0
             at = jnp.where(match, (side - 1) * TAKE + count, (NX - 1) * TAKE)
-            rows[at] = dz * PART + entry * PAGE
+            rows[at] = dz * CODES + entry * PAGE
             marks[at] = dz * EXPORT + entry
             return count + match.astype(jnp.int32)
 
@@ -473,38 +485,42 @@
     place = jnp.stack([tensor // 2, tensor % 2]).astype(jnp.int32)
 
     where = jnp.stack([myself // NX, myself % NX]).astype(jnp.int32)
-    flat_scales = kv_scales.astype(jnp.float32).reshape(-1)
-    part = export_pages(kv_codes, flat_scales, fork_export)
-    own = after(hidden.reshape(rows, width), part)
+    part = export_pages(kv_codes, kv_scales.transpose(2, 1, 0).reshape(2, OWN), fork_export)
+    own = after(hidden, part).reshape(rows, width)
     z = {0: part, 1: from_z(part, 1, "pages1"), -1: from_z(part, -1, "pages1")}
     aside = [from_y(own, d, "hidden") for d in (1, 2, 3)]
     w_far = from_core(w_out, "w_out")
     own_far = from_core(own, "hidden_core")
     z[2] = from_z(after(z[1], own_far, w_far), 1, "pages2")
     z[-2] = from_z(after(z[-1], own_far, w_far), -1, "pages2")
-    where = after(where, z[1], z[-1])
-    send_rows, send_marks, krow, vrow, mark = plan(where, fork_pull)
-    z[2], z[-2] = after(z[2], send_rows), after(z[-2], send_rows)
-    z[3], z[-3] = from_z(z[2], 1, "pages3"), from_z(z[-2], -1, "pages3")
-    z[4] = from_z(after(z[3], z[-3]), 1, "pages4")
-    parts = [own, *aside, own_far]
-    parts += [from_core(after(part, z[2], z[-2]), "hidden_core") for part in aside]
-    column = [z[d] for d in (0, 1, 2, 3, 4, -3, -2, -1)]
-    column[0] = after(column[0], *parts)
-
-    def sides(plus, across, minus, name):
-        return [from_x(minus, 1, name), from_x(across, 2, name), from_x(plus, -1, name)]
-
-    packed = pack(0, send_rows, send_marks, column)
-    keys = column + sides(*packed, "key_side")
-
     half = HD // 2
     freq = jnp.exp(-(2.0 * jnp.arange(half).astype(jnp.float32) / HD) * math.log(500000.0))
-    positions = (lengths[:, None] + jnp.arange(steps, dtype=jnp.int32)[None, :]).reshape(-1)
+    positions = (after(lengths, z[1], z[-1])[:, None] + jnp.arange(steps, dtype=jnp.int32)[None, :]).reshape(-1)
     angle = positions.astype(jnp.float32)[:, None] * freq[None, :]
     cos, sin = jnp.cos(angle), jnp.sin(angle)
     cosine = jnp.concatenate([cos, cos], axis=1)
     sine = jnp.concatenate([-sin, sin], axis=1)
+    z[2], z[-2] = after(z[2], cosine, sine), after(z[-2], cosine, sine)
+    z[3], z[-3] = from_z(z[2], 1, "pages3"), from_z(z[-2], -1, "pages3")
+    z[4] = from_z(after(z[3], z[-3]), 1, "pages4")
+    where = after(where, z[3], z[-3])
+    send_rows, send_marks, krow, vrow, mark = plan(where, fork_pull)
+    plus_far, across_far = [
+        from_core(after(aside[i], z[2], z[-2]), "hidden_core") for i in (0, 1)
+    ]
+    column = [z[d] for d in (0, 1, 2, 3, 4, -3, -2, -1)]
+    column[0] = after(column[0], plus_far, across_far)
+
+    def sides(plus, across, minus, name):
+        return [from_x(minus, 1, name), from_x(across, 2, name), from_x(plus, -1, name)]
+
+    packed = pack(0, send_rows, send_marks, column)
+    keys = column + sides(*packed, "key_side")
+    minus_far = from_core(after(aside[2], *packed), "hidden_core")
+    column[0] = after(column[0], *packed, minus_far)
+    plus, across, minus = pack(1, send_rows, send_marks, column)
+    parts = [own, *aside, own_far, plus_far, across_far, minus_far]
+
     q, k_new, v_new = project(
         place, parts, gain.reshape(2 * NY, width), w_query, w_keyval, cosine, sine
     )
@@ -515,19 +531,17 @@
     )
     table = page_table.reshape(-1)
 
-    column[0] = after(column[0], q)
-    plus, across, minus = pack(1, send_rows, send_marks, column)
+    across = after(across, q)
     values = column + sides(plus, across, minus, "value_side")
     values = values + [kv_codes[:, 1].reshape(OWN * PAGE, HD)]
     weights, fresh = score(table, krow, mark, lengths, q, k_new, v_new, own_scales, keys)
     attended = value(0, branches, table, vrow, weights, fresh, values)
     other = from_core(attended, "attended_core")
-    total, plus, across, minus = mix(place, attended, other, w_out, w_far)
-    got = [
-        from_y(across, -2, "output"),
-        from_y(plus, -1, "output"),
-        from_y(minus, -3, "output"),
-    ]
+    (across,) = mix((2,), place, attended, other, w_out, w_far)
+    got = [from_y(across, 2, "output_across")]
+    attended = after(attended, across)
+    total, plus, minus = mix((0, 1, 3), place, attended, other, w_out, w_far)
+    got += [from_y(plus, -1, "output"), from_y(minus, 1, "output")]
     total = total.astype(jnp.float32)
     for piece in got:
         total = total + piece.astype(jnp.float32)

time: 154 us -> 146 us (0.948); the launches traced: 151 us -> 145 us
  starting transfers between devices: 38 us -> 32.3 us
  Pallas kernels: 40.9 us -> 43.1 us
  local copies, waits for them, and re-layouts: 16.7 us -> 14.5 us
    ppermute x7, starting transfers between devices: 15.1 us -> 11.4 us  [from_z(): return lax.ppermute(value, 'branch', perm)]
    pallas_call x1 -> x2, Pallas kernels: 4.54 us -> 6.92 us  [mix(): pl.pallas_call(functools.partial(mix_kernel, blocks), out_shape=(out,) *...]
    ppermute x6, waiting for transfers between devices: 10.6 us -> 12.9 us  [from_x(): return lax.ppermute(value, 'branch', perm)]
    ppermute x6, waiting for transfers between devices: 29.3 us -> 27.1 us  [from_y(): return lax.ppermute(value, 'tensor', perm)]
    unnamed x63 -> x65, local copies, waits for them, and re-layouts: 10.2 us -> 10.2 us
  transfers between devices with their start and end apart: 25 -> 25, of which waited for: 12 -> 11; matrix products, arithmetic and copies ran while one was open for 5% -> 4% of each run, Pallas kernels for 18% -> 21%
where the time goes in v1:
time: 146 us; the launch traced here: 145 us
  waiting for transfers between devices  52 us (36%)
  Pallas kernels  43.1 us (30%)
  starting transfers between devices  32.3 us (22%)
  local copies, waits for them, and re-layouts  14.5 us (10%)
  other arithmetic  2.9 us (2%)
    ppermute x6, waiting for transfers between devices, from_y(): return lax.ppermute(value, 'tensor', perm)  27.1 us
    ppermute x6, waiting for transfers between devices, from_x(): return lax.ppermute(value, 'branch', perm)  12.9 us
    ppermute x6, starting transfers between devices, from_y(): return lax.ppermute(value, 'tensor', perm)  11.7 us
    ppermute x7, starting transfers between devices, from_z(): return lax.ppermute(value, 'branch', perm)  11.4 us
    pallas_call x1, Pallas kernels, score(): pl.pallas_call(functools.partial(score_kernel, count, len(keys)), out_sha...  10.9 us
    unnamed x65, local copies, waits for them, and re-layouts  10.2 us
    ppermute x7, waiting for transfers between devices, from_z(): return lax.ppermute(value, 'branch', perm)  10.1 us
    ppermute x6, starting transfers between devices, from_x(): return lax.ppermute(value, 'branch', perm)  7.92 us
  transfers between devices with their start and end apart: 25, of which 11 were waited for; matrix products, arithmetic and copies ran while one was open for 4% of the time, Pallas kernels for 21%

profile of v1, /device:TPU:2, one launch (start us, length us, event | category | flops | bytes accessed | tf_op | source)
XLA Modules:
  0.0 145.4 jit_solution(373006173716996164)
XLA Ops:
  0.0 2.6 %export_pages.1.refs_0_ = bf16[1040,128]{1,0:T(8,128)(2,1)} custom-call(s32[8]{0:T(128)} %picks.1, bf16[2,32]{1,0:T(2,128)(2,1)} %bitcast.14, bf16[32,2,64,128]{3,2,1,0:T(8,128)(2,1)} %codes.1), custom_call_target="tpu_custom_call" | custom-call | tf_op jit(solution)/shard_map/export_pages/pallas_call | solution.py:89
  4.2 1.9 %collective-permute-start.4 = (bf16[1040,128]{1,0:T(8,128)(2,1)}, bf16[1040,128]{1,0:T(8,128)(2,1)S(1)}, u32[]{:S(2)}, u32[]{:S(2)}) collective-permute-start(bf16[1040,128]{1,0:T(8,128)(2,1)} %export_pages.1.refs_0_), channel_id=1, source_target_pairs={{0,32},{8,40},{16,48},{24,56},{32,64},{40,72},{48,80},{56,88},{64,... | collective-permute-start | bytes 798728 | tf_op jit(solution)/shard_map/pages1/ppermute | solution.py:41
  6.1 3.9 %collective-permute-start = (bf16[1040,128]{1,0:T(8,128)(2,1)}, bf16[1040,128]{1,0:T(8,128)(2,1)S(1)}, u32[]{:S(2)}, u32[]{:S(2)}) collective-permute-start(bf16[1040,128]{1,0:T(8,128)(2,1)} %export_pages.1.refs_0_), channel_id=1, source_target_pairs={{0,224},{8,232},{16,240},{24,248},{32,0},{40,8},{48,16},{56,24},{6... | collective-permute-start | bytes 798728 | tf_op jit(solution)/shard_map/pages1/ppermute | solution.py:41
  10.1 3.2 %collective-permute-start.9 = (bf16[512,512]{1,0:T(8,128)(2,1)S(1)}, bf16[512,512]{1,0:T(8,128)(2,1)}, u32[]{:S(2)}, u32[]{:S(2)}) collective-permute-start(bf16[512,512]{1,0:T(8,128)(2,1)S(1)} %reshape.46.refs_0_), channel_id=1, source_target_pairs={{0,4},{1,5},{2,6},{3,7},{4,0},{5,1},{6,2},{7,3},{8,12},{9,13},{10,... | collective-permute-start | bytes 1572872 | tf_op jit(solution)/shard_map/hidden/ppermute | solution.py:53
  13.3 3.7 %collective-permute-done.4.refs_7_ = bf16[1040,128]{1,0:T(8,128)(2,1)S(1)} collective-permute-done((bf16[1040,128]{1,0:T(8,128)(2,1)}, bf16[1040,128]{1,0:T(8,128)(2,1)S(1)}, u32[]{:S(2)}, u32[]{:S(2)}) %collective-permute-start.4) | collective-permute-done | bytes 266272 | tf_op jit(solution)/shard_map/pages1/ppermute | solution.py:41
  17.0 3.0 %collective-permute-start.8 = (bf16[512,512]{1,0:T(8,128)(2,1)S(1)}, bf16[512,512]{1,0:T(8,128)(2,1)}, u32[]{:S(2)}, u32[]{:S(2)}) collective-permute-start(bf16[512,512]{1,0:T(8,128)(2,1)S(1)} %reshape.46.refs_0_), channel_id=1, source_target_pairs={{0,6},{1,7},{2,0},{3,1},{4,2},{5,3},{6,4},{7,5},{8,14},{9,15},{10,... | collective-permute-start | bytes 1572872 | tf_op jit(solution)/shard_map/hidden/ppermute | solution.py:53
  21.7 1.7 %collective-permute-start.3 = (bf16[1040,128]{1,0:T(8,128)(2,1)S(1)}, bf16[1040,128]{1,0:T(8,128)(2,1)S(1)}, u32[]{:S(2)}, u32[]{:S(2)}) collective-permute-start(bf16[1040,128]{1,0:T(8,128)(2,1)S(1)} %collective-permute-done.refs_1_), channel_id=1, source_target_pairs={{0,224},{8,232},{16,240},{24,248},{32,0},{40,8},{48,16},{56,24},{6... | collective-permute-start | bytes 798728 | tf_op jit(solution)/shard_map/pages2/ppermute | solution.py:41
  24.9 4.5 %collective-permute-done.3.refs_2_ = bf16[1040,128]{1,0:T(8,128)(2,1)S(1)} collective-permute-done((bf16[1040,128]{1,0:T(8,128)(2,1)S(1)}, bf16[1040,128]{1,0:T(8,128)(2,1)S(1)}, u32[]{:S(2)}, u32[]{:S(2)}) %collective-permute-start.3) | collective-permute-done | bytes 266272 | tf_op jit(solution)/shard_map/pages2/ppermute | solution.py:41
  29.4 2.6 %collective-permute-start.5 = (bf16[1040,128]{1,0:T(8,128)(2,1)S(1)}, bf16[1040,128]{1,0:T(8,128)(2,1)S(1)}, u32[]{:S(2)}, u32[]{:S(2)}) collective-permute-start(bf16[1040,128]{1,0:T(8,128)(2,1)S(1)} %collective-permute-done.3.refs_2_), channel_id=1, source_target_pairs={{0,224},{8,232},{16,240},{24,248},{32,0},{40,8},{48,16},{56,24},{6... | collective-permute-start | bytes 798728 | tf_op jit(solution)/shard_map/pages3/ppermute | solution.py:41
  32.1 4.9 %collective-permute-done.8.refs_1_ = bf16[512,512]{1,0:T(8,128)(2,1)} collective-permute-done((bf16[512,512]{1,0:T(8,128)(2,1)S(1)}, bf16[512,512]{1,0:T(8,128)(2,1)}, u32[]{:S(2)}, u32[]{:S(2)}) %collective-permute-start.8) | collective-permute-done | bytes 524320 | tf_op jit(solution)/shard_map/hidden/ppermute | solution.py:53
  37.5 1.2 collective-permute-start.10
  41.8 4.1 %plan.1 = (s32[97]{0:T(128)}, s32[97]{0:T(128)}, s32[96]{0:T(128)}, s32[96]{0:T(128)}, s32[96]{0:T(128)}) custom-call(s32[2]{0:T(128)} %pad_add_fusion.1.where, s32[2048]{0:T(1024)} %reshape.47.pull), custom_call_target="tpu_custom_call" | custom-call | tf_op jit(solution)/shard_map/plan/pallas_call | solution.py:459
  47.6 3.4 %pack.2 = (bf16[2112,128]{1,0:T(8,128)(2,1)}, bf16[2112,128]{1,0:T(8,128)(2,1)}, bf16[2112,128]{1,0:T(8,128)(2,1)}) custom-call(s32[97]{0:T(128)} %get-tuple-element.51.rows, s32[97]{0:T(128)} %get-tuple-element.52.marks, bf16[1040,128]{1,0:T(8,128)(2,1)} %export_pages.1.refs_0_, bf16[1040,128]{1,0:T(8,128)(2,1)} %copy-done.4, bf16[1040,128]{1,0:T(8,128)(2,1)} %copy-done.6, ...), custom_call_target="tpu_custom_call" | custom-call | tf_op jit(solution)/shard_map/pack/pallas_call | solution.py:132
  51.0 1.7 %collective-permute-start.17 = (bf16[2112,128]{1,0:T(8,128)(2,1)}, bf16[2112,128]{1,0:T(8,128)(2,1)}, u32[]{:S(2)}, u32[]{:S(2)}) collective-permute-start(bf16[2112,128]{1,0:T(8,128)(2,1)} %get-tuple-element.55), channel_id=1, source_target_pairs={{0,8},{8,16},{16,24},{24,0},{32,40},{40,48},{48,56},{56,32},{64,72... | collective-permute-start | bytes 1622024 | tf_op jit(solution)/shard_map/key_side/ppermute | solution.py:47
  52.8 2.1 %collective-permute-start.16 = (bf16[2112,128]{1,0:T(8,128)(2,1)}, bf16[2112,128]{1,0:T(8,128)(2,1)}, u32[]{:S(2)}, u32[]{:S(2)}) collective-permute-start(bf16[2112,128]{1,0:T(8,128)(2,1)} %get-tuple-element.56), channel_id=1, source_target_pairs={{0,16},{8,24},{16,0},{24,8},{32,48},{40,56},{48,32},{56,40},{64,80... | collective-permute-start | bytes 1622024 | tf_op jit(solution)/shard_map/key_side/ppermute | solution.py:47
  54.8 1.4 collective-permute-start.15
  57.2 3.3 %pack.3 = (bf16[2048,128]{1,0:T(8,128)(2,1)}, bf16[2048,128]{1,0:T(8,128)(2,1)}, bf16[2048,128]{1,0:T(8,128)(2,1)}) custom-call(s32[97]{0:T(128)} %get-tuple-element.51.rows, s32[97]{0:T(128)} %get-tuple-element.52.marks, bf16[1040,128]{1,0:T(8,128)(2,1)} %export_pages.1.refs_0_, bf16[1040,128]{1,0:T(8,128)(2,1)} %copy-done.4, bf16[1040,128]{1,0:T(8,128)(2,1)} %copy-done.6, ...), custom_call_target="tpu_custom_call" | custom-call | tf_op jit(solution)/shard_map/pack/pallas_call | solution.py:132
  60.5 2.2 %copy-done.16 = bf16[4096,512]{1,0:T(8,128)(2,1)S(1)} copy-done((bf16[4096,512]{1,0:T(8,128)(2,1)S(1)}, bf16[4096,512]{1,0:T(8,128)(2,1)}, u32[]{:S(2)}) %copy-start.16) | copy-done | bytes 4194328
  62.7 1.6 %copy-done.17 = bf16[2,4096,128]{2,1,0:T(8,128)(2,1)S(1)} copy-done((bf16[2,4096,128]{2,1,0:T(8,128)(2,1)S(1)}, bf16[2,4096,128]{2,1,0:T(8,128)(2,1)}, u32[]{:S(2)}) %copy-start.17) | copy-done | bytes 2097176
  66.5 6.6 %project.1 = (bf16[2048,128]{1,0:T(8,128)(2,1)S(1)}, bf16[512,128]{1,0:T(8,128)(2,1)S(1)}, bf16[512,128]{1,0:T(8,128)(2,1)S(1)}) custom-call(s32[2]{0:T(128)S(1)} %pad_add_fusion.place, bf16[512,512]{1,0:T(8,128)(2,1)S(1)} %reshape.46.refs_0_, bf16[512,512]{1,0:T(8,128)(2,1)} %collective-permute-done.8.refs_1_, ...), custom_call_target="tpu_custom_call" | custom-call | tf_op jit(solution)/shard_map/project/pallas_call | solution.py:186
  74.5 2.1 %collective-permute-start.18 = (bf16[2048,128]{1,0:T(8,128)(2,1)}, bf16[2048,128]{1,0:T(8,128)(2,1)S(1)}, u32[]{:S(2)}, u32[]{:S(2)}) collective-permute-start(bf16[2048,128]{1,0:T(8,128)(2,1)} %get-tuple-element.65), channel_id=1, source_target_pairs={{0,24},{8,0},{16,8},{24,16},{32,56},{40,32},{48,40},{56,48},{64,88... | collective-permute-start | bytes 1572872 | tf_op jit(solution)/shard_map/value_side/ppermute | solution.py:47
  76.9 1.3 fusion.1
  78.2 3.1 %collective-permute-done.15.refs_8_ = bf16[2112,128]{1,0:T(8,128)(2,1)} collective-permute-done((bf16[2112,128]{1,0:T(8,128)(2,1)}, bf16[2112,128]{1,0:T(8,128)(2,1)}, u32[]{:S(2)}, u32[]{:S(2)}) %collective-permute-start.15) | collective-permute-done | bytes 540704 | tf_op jit(solution)/shard_map/key_side/ppermute | solution.py:47
  82.5 10.9 %score.1 = (bf16[2048,512]{1,0:T(8,128)(2,1)S(1)}, f32[2048,128]{1,0:T(8,128)S(1)}) custom-call(s32[1024]{0:T(1024)S(1)} %reshape.44.table, s32[96]{0:T(128)S(1)} %copy-done.26, s32[96]{0:T(128)S(1)} %copy-done.27, s32[128]{0:T(128)S(1)} %copy-done.24, bf16[2048,128]{1,0:T(8,128)(2,1)S(1)} %copy-done.23, bf16[512,128]{1,0:T(8,128)(2,1)S(1)} %get-tuple-element.60.k_new, ...), custom_call_target="tpu_custom_call" | custom-call | tf_op jit(solution)/shard_map/score/pallas_call | solution.py:307
  93.5 9.7 %collective-permute-done.18.refs_8_ = bf16[2048,128]{1,0:T(8,128)(2,1)S(1)} collective-permute-done((bf16[2048,128]{1,0:T(8,128)(2,1)}, bf16[2048,128]{1,0:T(8,128)(2,1)S(1)}, u32[]{:S(2)}, u32[]{:S(2)}) %collective-permute-start.18) | collective-permute-done | bytes 524320 | tf_op jit(solution)/shard_map/value_side/ppermute | solution.py:47
  103.2 5.3 %value.1.near = bf16[512,512]{1,0:T(8,128)(2,1)S(1)} custom-call(s32[1024]{0:T(1024)S(1)} %reshape.44.table, s32[96]{0:T(128)S(1)} %copy-done.25, bf16[2048,512]{1,0:T(8,128)(2,1)S(1)} %get-tuple-element.62.weights, f32[2048,128]{1,0:T(8,128)S(1)} %get-tuple-element.63.fresh, bf16[1040,128]{1,0:T(8,128)(2,1)S(1)} %copy-done.1, ...), custom_call_target="tpu_custom_call" | custom-call | tf_op jit(solution)/shard_map/value/pallas_call | solution.py:354
  108.9 1.9 %collective-permute-done.21.far = bf16[512,512]{1,0:T(8,128)(2,1)S(1)} collective-permute-done((bf16[512,512]{1,0:T(8,128)(2,1)S(1)}, bf16[512,512]{1,0:T(8,128)(2,1)S(1)}, u32[]{:S(2)}, u32[]{:S(2)}) %collective-permute-start.21) | collective-permute-done | bytes 524320 | tf_op jit(solution)/shard_map/attended_core/ppermute | solution.py:58
  110.7 2.9 %mix.2 = bf16[512,512]{1,0:T(8,128)(2,1)S(1)} custom-call(s32[2]{0:T(128)S(1)} %pad_add_fusion.place, bf16[512,512]{1,0:T(8,128)(2,1)S(1)} %value.1.near, bf16[512,512]{1,0:T(8,128)(2,1)S(1)} %collective-permute-done.21.far, bf16[512,4096]{1,0:T(8,128)(2,1)S(1)} %copy-done, bf16[512,4096]{1,0:T(8,128)(2,1)} %collective-permute-done.2.w_far), custom_call_target="tpu_custom_call" | custom-call | tf_op jit(solution)/shard_map/mix/pallas_call | solution.py:389
  113.7 4.0 %mix.3 = (bf16[512,512]{1,0:T(8,128)(2,1)S(1)}, bf16[512,512]{1,0:T(8,128)(2,1)S(1)}, bf16[512,512]{1,0:T(8,128)(2,1)S(1)}) custom-call(s32[2]{0:T(128)S(1)} %pad_add_fusion.place, bf16[512,512]{1,0:T(8,128)(2,1)S(1)} %value.1.near, bf16[512,512]{1,0:T(8,128)(2,1)S(1)} %collective-permute-done.21.far, bf16[512,4096]{1,0:T(8,128)(2,1)S(1)} %copy-done, ...), custom_call_target="tpu_custom_call" | custom-call | tf_op jit(solution)/shard_map/mix/pallas_call | solution.py:389
  118.0 3.0 %collective-permute-start.24 = (bf16[512,512]{1,0:T(8,128)(2,1)S(1)}, bf16[512,512]{1,0:T(8,128)(2,1)S(1)}, u32[]{:S(2)}, u32[]{:S(2)}) collective-permute-start(bf16[512,512]{1,0:T(8,128)(2,1)S(1)} %get-tuple-element.72), channel_id=1, source_target_pairs={{0,6},{1,7},{2,0},{3,1},{4,2},{5,3},{6,4},{7,5},{8,14},{9,15},{10,... | collective-permute-start | bytes 1572872 | tf_op jit(solution)/shard_map/output/ppermute | solution.py:53
  122.0 11.7 %collective-permute-done.23 = bf16[512,512]{1,0:T(8,128)(2,1)S(1)} collective-permute-done((bf16[512,512]{1,0:T(8,128)(2,1)S(1)}, bf16[512,512]{1,0:T(8,128)(2,1)S(1)}, u32[]{:S(2)}, u32[]{:S(2)}) %collective-permute-start.23) | collective-permute-done | bytes 524320 | tf_op jit(solution)/shard_map/output/ppermute | solution.py:53
  133.7 9.7 %collective-permute-done.24 = bf16[512,512]{1,0:T(8,128)(2,1)S(1)} collective-permute-done((bf16[512,512]{1,0:T(8,128)(2,1)S(1)}, bf16[512,512]{1,0:T(8,128)(2,1)S(1)}, u32[]{:S(2)}, u32[]{:S(2)}) %collective-permute-start.24) | collective-permute-done | bytes 524320 | tf_op jit(solution)/shard_map/output/ppermute | solution.py:53
  (108 shorter events, 19.5 us)
Async XLA Ops:
  0.0 40.5 %copy-start.28 = (s32[32,64]{1,0:T(8,128)S(1)}, s32[32,64]{1,0:T(8,128)}, u32[]{:S(2)}) copy-start(s32[32,64]{1,0:T(8,128)} %param.19) | copy-start | bytes 24580
  0.0 56.3 %copy-start.29 = (f32[4096]{0:T(1024)S(1)}, f32[4096]{0:T(1024)}, u32[]{:S(2)}) copy-start(f32[4096]{0:T(1024)} %param.12) | copy-start | bytes 49156
  0.0 21.6 %collective-permute-start.2 = (bf16[512,4096]{1,0:T(8,128)(2,1)}, bf16[512,4096]{1,0:T(8,128)(2,1)}, u32[]{:S(2)}, u32[]{:S(2)}) collective-permute-start(bf16[512,4096]{1,0:T(8,128)(2,1)} %w_near.3), channel_id=1, source_target_pairs={{0,1},{1,0},{2,3},{3,2},{4,5},{5,4},{6,7},{7,6},{8,9},{9,8},{10,11... | collective-permute-start | bytes 12582920 | tf_op jit(solution)/shard_map/w_out/ppermute | solution.py:58
  3.8 17.1 %collective-permute-start.1 = (bf16[512,512]{1,0:T(8,128)(2,1)S(1)}, bf16[512,512]{1,0:T(8,128)(2,1)S(1)}, u32[]{:S(2)}, u32[]{:S(2)}) collective-permute-start(bf16[512,512]{1,0:T(8,128)(2,1)S(1)} %reshape.46.refs_0_), channel_id=1, source_target_pairs={{0,1},{1,0},{2,3},{3,2},{4,5},{5,4},{6,7},{7,6},{8,9},{9,8},{10,11... | collective-permute-start | bytes 1572872 | tf_op jit(solution)/shard_map/hidden_core/ppermute | solution.py:58
  4.2 12.8 %collective-permute-start.4 = (bf16[1040,128]{1,0:T(8,128)(2,1)}, bf16[1040,128]{1,0:T(8,128)(2,1)S(1)}, u32[]{:S(2)}, u32[]{:S(2)}) collective-permute-start(bf16[1040,128]{1,0:T(8,128)(2,1)} %export_pages.1.refs_0_), channel_id=1, source_target_pairs={{0,32},{8,40},{16,48},{24,56},{32,64},{40,72},{48,80},{56,88},{64,... | collective-permute-start | bytes 798728 | tf_op jit(solution)/shard_map/pages1/ppermute | solution.py:41
  6.1 13.9 %collective-permute-start = (bf16[1040,128]{1,0:T(8,128)(2,1)}, bf16[1040,128]{1,0:T(8,128)(2,1)S(1)}, u32[]{:S(2)}, u32[]{:S(2)}) collective-permute-start(bf16[1040,128]{1,0:T(8,128)(2,1)} %export_pages.1.refs_0_), channel_id=1, source_target_pairs={{0,224},{8,232},{16,240},{24,248},{32,0},{40,8},{48,16},{56,24},{6... | collective-permute-start | bytes 798728 | tf_op jit(solution)/shard_map/pages1/ppermute | solution.py:41
  10.1 22.0 %collective-permute-start.9 = (bf16[512,512]{1,0:T(8,128)(2,1)S(1)}, bf16[512,512]{1,0:T(8,128)(2,1)}, u32[]{:S(2)}, u32[]{:S(2)}) collective-permute-start(bf16[512,512]{1,0:T(8,128)(2,1)S(1)} %reshape.46.refs_0_), channel_id=1, source_target_pairs={{0,4},{1,5},{2,6},{3,7},{4,0},{5,1},{6,2},{7,3},{8,12},{9,13},{10,... | collective-permute-start | bytes 1572872 | tf_op jit(solution)/shard_map/hidden/ppermute | solution.py:53
  17.0 29.9 %copy-start.2 = (bf16[1040,128]{1,0:T(8,128)(2,1)}, bf16[1040,128]{1,0:T(8,128)(2,1)S(1)}, u32[]{:S(2)}) copy-start(bf16[1040,128]{1,0:T(8,128)(2,1)S(1)} %collective-permute-done.4.refs_7_) | copy-start | bytes 798724
  17.0 20.0 %collective-permute-start.8 = (bf16[512,512]{1,0:T(8,128)(2,1)S(1)}, bf16[512,512]{1,0:T(8,128)(2,1)}, u32[]{:S(2)}, u32[]{:S(2)}) collective-permute-start(bf16[512,512]{1,0:T(8,128)(2,1)S(1)} %reshape.46.refs_0_), channel_id=1, source_target_pairs={{0,6},{1,7},{2,0},{3,1},{4,2},{5,3},{6,4},{7,5},{8,14},{9,15},{10,... | collective-permute-start | bytes 1572872 | tf_op jit(solution)/shard_map/hidden/ppermute | solution.py:53
  20.0 26.9 %copy-start.4 = (bf16[1040,128]{1,0:T(8,128)(2,1)}, bf16[1040,128]{1,0:T(8,128)(2,1)S(1)}, u32[]{:S(2)}) copy-start(bf16[1040,128]{1,0:T(8,128)(2,1)S(1)} %collective-permute-done.refs_1_) | copy-start | bytes 798724
  21.7 7.8 %collective-permute-start.3 = (bf16[1040,128]{1,0:T(8,128)(2,1)S(1)}, bf16[1040,128]{1,0:T(8,128)(2,1)S(1)}, u32[]{:S(2)}, u32[]{:S(2)}) collective-permute-start(bf16[1040,128]{1,0:T(8,128)(2,1)S(1)} %collective-permute-done.refs_1_), channel_id=1, source_target_pairs={{0,224},{8,232},{16,240},{24,248},{32,0},{40,8},{48,16},{56,24},{6... | collective-permute-start | bytes 798728 | tf_op jit(solution)/shard_map/pages2/ppermute | solution.py:41
  23.4 8.7 %collective-permute-start.6 = (bf16[1040,128]{1,0:T(8,128)(2,1)S(1)}, bf16[1040,128]{1,0:T(8,128)(2,1)S(1)}, u32[]{:S(2)}, u32[]{:S(2)}) collective-permute-start(bf16[1040,128]{1,0:T(8,128)(2,1)S(1)} %collective-permute-done.4.refs_7_), channel_id=1, source_target_pairs={{0,32},{8,40},{16,48},{24,56},{32,64},{40,72},{48,80},{56,88},{64,... | collective-permute-start | bytes 798728 | tf_op jit(solution)/shard_map/pages2/ppermute | solution.py:41
  29.4 17.5 %copy-start.6 = (bf16[1040,128]{1,0:T(8,128)(2,1)}, bf16[1040,128]{1,0:T(8,128)(2,1)S(1)}, u32[]{:S(2)}) copy-start(bf16[1040,128]{1,0:T(8,128)(2,1)S(1)} %collective-permute-done.3.refs_2_) | copy-start | bytes 798724
  29.4 9.3 %collective-permute-start.5 = (bf16[1040,128]{1,0:T(8,128)(2,1)S(1)}, bf16[1040,128]{1,0:T(8,128)(2,1)S(1)}, u32[]{:S(2)}, u32[]{:S(2)}) collective-permute-start(bf16[1040,128]{1,0:T(8,128)(2,1)S(1)} %collective-permute-done.3.refs_2_), channel_id=1, source_target_pairs={{0,224},{8,232},{16,240},{24,248},{32,0},{40,8},{48,16},{56,24},{6... | collective-permute-start | bytes 798728 | tf_op jit(solution)/shard_map/pages3/ppermute | solution.py:41
  32.1 7.6 %collective-permute-start.7 = (bf16[1040,128]{1,0:T(8,128)(2,1)S(1)}, bf16[1040,128]{1,0:T(8,128)(2,1)S(1)}, u32[]{:S(2)}, u32[]{:S(2)}) collective-permute-start(bf16[1040,128]{1,0:T(8,128)(2,1)S(1)} %collective-permute-done.6.refs_6_), channel_id=1, source_target_pairs={{0,32},{8,40},{16,48},{24,56},{32,64},{40,72},{48,80},{56,88},{64,... | collective-permute-start | bytes 798728 | tf_op jit(solution)/shard_map/pages3/ppermute | solution.py:41
  37.0 8.9 %collective-permute-start.11 = (bf16[512,512]{1,0:T(8,128)(2,1)}, bf16[512,512]{1,0:T(8,128)(2,1)}, u32[]{:S(2)}, u32[]{:S(2)}) collective-permute-start(bf16[512,512]{1,0:T(8,128)(2,1)} %collective-permute-done.8.refs_1_), channel_id=1, source_target_pairs={{0,1},{1,0},{2,3},{3,2},{4,5},{5,4},{6,7},{7,6},{8,9},{9,8},{10,11... | collective-permute-start | bytes 1572872 | tf_op jit(solution)/shard_map/hidden_core/ppermute | solution.py:58
  37.0 8.9 %collective-permute-start.12 = (bf16[512,512]{1,0:T(8,128)(2,1)}, bf16[512,512]{1,0:T(8,128)(2,1)}, u32[]{:S(2)}, u32[]{:S(2)}) collective-permute-start(bf16[512,512]{1,0:T(8,128)(2,1)} %collective-permute-done.9.refs_2_), channel_id=1, source_target_pairs={{0,1},{1,0},{2,3},{3,2},{4,5},{5,4},{6,7},{7,6},{8,9},{9,8},{10,11... | collective-permute-start | bytes 1572872 | tf_op jit(solution)/shard_map/hidden_core/ppermute | solution.py:58
  37.5 15.2 %collective-permute-start.10 = (bf16[512,512]{1,0:T(8,128)(2,1)S(1)}, bf16[512,512]{1,0:T(8,128)(2,1)}, u32[]{:S(2)}, u32[]{:S(2)}) collective-permute-start(bf16[512,512]{1,0:T(8,128)(2,1)S(1)} %reshape.46.refs_0_), channel_id=1, source_target_pairs={{0,2},{1,3},{2,4},{3,5},{4,6},{5,7},{6,0},{7,1},{8,10},{9,11},{10,... | collective-permute-start | bytes 1572872 | tf_op jit(solution)/shard_map/hidden/ppermute | solution.py:53
  39.7 7.2 %collective-permute-start.13 = (bf16[1040,128]{1,0:T(8,128)(2,1)S(1)}, bf16[1040,128]{1,0:T(8,128)(2,1)S(1)}, u32[]{:S(2)}, u32[]{:S(2)}) collective-permute-start(bf16[1040,128]{1,0:T(8,128)(2,1)S(1)} %collective-permute-done.5.refs_3_), channel_id=1, source_target_pairs={{0,224},{8,232},{16,240},{24,248},{32,0},{40,8},{48,16},{56,24},{6... | collective-permute-start | bytes 798728 | tf_op jit(solution)/shard_map/pages4/ppermute | solution.py:41
  51.0 25.6 %collective-permute-start.17 = (bf16[2112,128]{1,0:T(8,128)(2,1)}, bf16[2112,128]{1,0:T(8,128)(2,1)}, u32[]{:S(2)}, u32[]{:S(2)}) collective-permute-start(bf16[2112,128]{1,0:T(8,128)(2,1)} %get-tuple-element.55), channel_id=1, source_target_pairs={{0,8},{8,16},{16,24},{24,0},{32,40},{40,48},{48,56},{56,32},{64,72... | collective-permute-start | bytes 1622024 | tf_op jit(solution)/shard_map/key_side/ppermute | solution.py:47
  52.7 3.6 %collective-permute-start.14 = (bf16[512,512]{1,0:T(8,128)(2,1)}, bf16[512,512]{1,0:T(8,128)(2,1)S(1)}, u32[]{:S(2)}, u32[]{:S(2)}) collective-permute-start(bf16[512,512]{1,0:T(8,128)(2,1)} %collective-permute-done.10.refs_3_), channel_id=1, source_target_pairs={{0,1},{1,0},{2,3},{3,2},{4,5},{5,4},{6,7},{7,6},{8,9},{9,8},{10,11... | collective-permute-start | bytes 1572872 | tf_op jit(solution)/shard_map/hidden_core/ppermute | solution.py:58
  52.8 25.4 %collective-permute-start.16 = (bf16[2112,128]{1,0:T(8,128)(2,1)}, bf16[2112,128]{1,0:T(8,128)(2,1)}, u32[]{:S(2)}, u32[]{:S(2)}) collective-permute-start(bf16[2112,128]{1,0:T(8,128)(2,1)} %get-tuple-element.56), channel_id=1, source_target_pairs={{0,16},{8,24},{16,0},{24,8},{32,48},{40,56},{48,32},{56,40},{64,80... | collective-permute-start | bytes 1622024 | tf_op jit(solution)/shard_map/key_side/ppermute | solution.py:47
  54.8 26.5 %collective-permute-start.15 = (bf16[2112,128]{1,0:T(8,128)(2,1)}, bf16[2112,128]{1,0:T(8,128)(2,1)}, u32[]{:S(2)}, u32[]{:S(2)}) collective-permute-start(bf16[2112,128]{1,0:T(8,128)(2,1)} %get-tuple-element.57), channel_id=1, source_target_pairs={{0,24},{8,0},{16,8},{24,16},{32,56},{40,32},{48,40},{56,48},{64,88... | collective-permute-start | bytes 1622024 | tf_op jit(solution)/shard_map/key_side/ppermute | solution.py:47
  73.9 29.3 %copy-start.25 = (s32[96]{0:T(128)S(1)}, s32[96]{0:T(128)}, u32[]{:S(2)}) copy-start(s32[96]{0:T(128)} %get-tuple-element.46.vrow) | copy-start | bytes 1156
  73.9 19.6 %collective-permute-start.19 = (bf16[2048,128]{1,0:T(8,128)(2,1)}, bf16[2048,128]{1,0:T(8,128)(2,1)S(1)}, u32[]{:S(2)}, u32[]{:S(2)}) collective-permute-start(bf16[2048,128]{1,0:T(8,128)(2,1)} %get-tuple-element.67), channel_id=1, source_target_pairs={{0,16},{8,24},{16,0},{24,8},{32,48},{40,56},{48,32},{56,40},{64,80... | collective-permute-start | bytes 1572872 | tf_op jit(solution)/shard_map/value_side/ppermute | solution.py:47
  74.5 28.7 %collective-permute-start.18 = (bf16[2048,128]{1,0:T(8,128)(2,1)}, bf16[2048,128]{1,0:T(8,128)(2,1)S(1)}, u32[]{:S(2)}, u32[]{:S(2)}) collective-permute-start(bf16[2048,128]{1,0:T(8,128)(2,1)} %get-tuple-element.65), channel_id=1, source_target_pairs={{0,24},{8,0},{16,8},{24,16},{32,56},{40,32},{48,40},{56,48},{64,88... | collective-permute-start | bytes 1572872 | tf_op jit(solution)/shard_map/value_side/ppermute | solution.py:47
  76.6 26.6 %collective-permute-start.20 = (bf16[2048,128]{1,0:T(8,128)(2,1)}, bf16[2048,128]{1,0:T(8,128)(2,1)}, u32[]{:S(2)}, u32[]{:S(2)}) collective-permute-start(bf16[2048,128]{1,0:T(8,128)(2,1)} %get-tuple-element.68), channel_id=1, source_target_pairs={{0,8},{8,16},{16,24},{24,0},{32,40},{40,48},{48,56},{56,32},{64,72... | collective-permute-start | bytes 1572872 | tf_op jit(solution)/shard_map/value_side/ppermute | solution.py:47
  93.4 17.3 %copy-start = (bf16[512,4096]{1,0:T(8,128)(2,1)S(1)}, bf16[512,4096]{1,0:T(8,128)(2,1)}, u32[]{:S(2)}) copy-start(bf16[512,4096]{1,0:T(8,128)(2,1)} %w_near.3) | copy-start | bytes 12582916
  108.5 2.2 %collective-permute-start.21 = (bf16[512,512]{1,0:T(8,128)(2,1)S(1)}, bf16[512,512]{1,0:T(8,128)(2,1)S(1)}, u32[]{:S(2)}, u32[]{:S(2)}) collective-permute-start(bf16[512,512]{1,0:T(8,128)(2,1)S(1)} %value.1.near), channel_id=1, source_target_pairs={{0,1},{1,0},{2,3},{3,2},{4,5},{5,4},{6,7},{7,6},{8,9},{9,8},{10,11... | collective-permute-start | bytes 1572872 | tf_op jit(solution)/shard_map/attended_core/ppermute | solution.py:58
  117.7 16.1 %collective-permute-start.23 = (bf16[512,512]{1,0:T(8,128)(2,1)S(1)}, bf16[512,512]{1,0:T(8,128)(2,1)S(1)}, u32[]{:S(2)}, u32[]{:S(2)}) collective-permute-start(bf16[512,512]{1,0:T(8,128)(2,1)S(1)} %get-tuple-element.71), channel_id=1, source_target_pairs={{0,2},{1,3},{2,4},{3,5},{4,6},{5,7},{6,0},{7,1},{8,10},{9,11},{10,... | collective-permute-start | bytes 1572872 | tf_op jit(solution)/shard_map/output/ppermute | solution.py:53
  118.0 25.4 %collective-permute-start.24 = (bf16[512,512]{1,0:T(8,128)(2,1)S(1)}, bf16[512,512]{1,0:T(8,128)(2,1)S(1)}, u32[]{:S(2)}, u32[]{:S(2)}) collective-permute-start(bf16[512,512]{1,0:T(8,128)(2,1)S(1)} %get-tuple-element.72), channel_id=1, source_target_pairs={{0,6},{1,7},{2,0},{3,1},{4,2},{5,3},{6,4},{7,5},{8,14},{9,15},{10,... | collective-permute-start | bytes 1572872 | tf_op jit(solution)/shard_map/output/ppermute | solution.py:53
  121.0 23.2 %collective-permute-start.22 = (bf16[512,512]{1,0:T(8,128)(2,1)S(1)}, bf16[512,512]{1,0:T(8,128)(2,1)S(1)}, u32[]{:S(2)}, u32[]{:S(2)}) collective-permute-start(bf16[512,512]{1,0:T(8,128)(2,1)S(1)} %mix.2), channel_id=1, source_target_pairs={{0,4},{1,5},{2,6},{3,7},{4,0},{5,1},{6,2},{7,3},{8,12},{9,13},{10,... | collective-permute-start | bytes 1572872 | tf_op jit(solution)/shard_map/output_across/ppermute | solution.py:53
  (25 other events, 225.8 us)

commit v2 on v1

--- a/solution.py
+++ b/solution.py
@@ -372,25 +372,25 @@
     )(table, vrow, weights, fresh, *values)
 
 
-def mix_kernel(blocks, place, near, far, w_near, w_far, *outs):
+def mix_kernel(place, near, far, w_near, w_far, *outs):
     y, c = place[0], place[1]
-    width = outs[0].shape[1]
-    for j, out in zip(blocks, outs):
+    half, width = outs[0].shape
+    for j in (2, 1, 3, 0):
         at = pl.ds(pl.multiple_of((lax.rem(y + j, NY) * 2 + c) * width, width), width)
         total = jnp.dot(near[...], w_near[:, at], preferred_element_type=jnp.float32)
         total += jnp.dot(far[...], w_far[:, at], preferred_element_type=jnp.float32)
-        out[...] = total.astype(jnp.bfloat16)
-
-
-def mix(blocks, place, near, far, w_near, w_far):
-    tokens = near.shape[0]
+        outs[2 * j][...] = total[:half].astype(jnp.bfloat16)
+        outs[2 * j + 1][...] = total[half:].astype(jnp.bfloat16)
+
+
+def mix(place, near, far, w_near, w_far):
     width = w_near.shape[1] // (2 * NY)
-    out = jax.ShapeDtypeStruct((tokens, width), jnp.bfloat16)
-    return pl.pallas_call(
-        functools.partial(mix_kernel, blocks),
-        out_shape=(out,) * len(blocks),
+    out = jax.ShapeDtypeStruct((near.shape[0] // 2, width), jnp.bfloat16)
+    return pl.pallas_call(
+        mix_kernel,
+        out_shape=(out,) * (2 * NY),
         in_specs=[spec(pltpu.SMEM)] + [spec(pltpu.VMEM)] * 4,
-        out_specs=(spec(pltpu.VMEM),) * len(blocks),
+        out_specs=(spec(pltpu.VMEM),) * (2 * NY),
         compiler_params=pltpu.CompilerParams(vmem_limit_bytes=LIMIT),
         name="mix",
     )(place, near, far, w_near, w_far)
@@ -490,9 +490,8 @@
     z = {0: part, 1: from_z(part, 1, "pages1"), -1: from_z(part, -1, "pages1")}
     aside = [from_y(own, d, "hidden") for d in (1, 2, 3)]
     w_far = from_core(w_out, "w_out")
-    own_far = from_core(own, "hidden_core")
-    z[2] = from_z(after(z[1], own_far, w_far), 1, "pages2")
-    z[-2] = from_z(after(z[-1], own_far, w_far), -1, "pages2")
+    z[2] = from_z(after(z[1], w_far), 1, "pages2")
+    z[-2] = from_z(after(z[-1], w_far), -1, "pages2")
     half = HD // 2
     freq = jnp.exp(-(2.0 * jnp.arange(half).astype(jnp.float32) / HD) * math.log(500000.0))
     positions = (after(lengths, z[1], z[-1])[:, None] + jnp.arange(steps, dtype=jnp.int32)[None, :]).reshape(-1)
@@ -517,7 +516,8 @@
     packed = pack(0, send_rows, send_marks, column)
     keys = column + sides(*packed, "key_side")
     minus_far = from_core(after(aside[2], *packed), "hidden_core")
-    column[0] = after(column[0], *packed, minus_far)
+    own_far = from_core(after(own, *packed), "hidden_core")
+    column[0] = after(column[0], *packed, minus_far, own_far)
     plus, across, minus = pack(1, send_rows, send_marks, column)
     parts = [own, *aside, own_far, plus_far, across_far, minus_far]
 
@@ -537,15 +537,25 @@
     weights, fresh = score(table, krow, mark, lengths, q, k_new, v_new, own_scales, keys)
     attended = value(0, branches, table, vrow, weights, fresh, values)
     other = from_core(attended, "attended_core")
-    (across,) = mix((2,), place, attended, other, w_out, w_far)
-    got = [from_y(across, 2, "output_across")]
-    attended = after(attended, across)
-    total, plus, minus = mix((0, 1, 3), place, attended, other, w_out, w_far)
-    got += [from_y(plus, -1, "output"), from_y(minus, 1, "output")]
-    total = total.astype(jnp.float32)
-    for piece in got:
-        total = total + piece.astype(jnp.float32)
-    return total.astype(jnp.bfloat16).reshape(branches, steps, width)
+    own_up, own_low, plus_up, plus_low, across_up, across_low, minus_up, minus_low = mix(
+        place, attended, other, w_out, w_far
+    )
+
+    def add(*terms):
+        total = terms[0].astype(jnp.float32)
+        for term in terms[1:]:
+            total = total + term.astype(jnp.float32)
+        return total.astype(jnp.bfloat16)
+
+    passed_up = from_y(across_up, -1, "output_relay")
+    passed_low = from_y(across_low, 1, "output_relay")
+    got_low = from_y(plus_low, -1, "output_near")
+    got_up = from_y(minus_up, 1, "output_near")
+    relayed_up = from_y(add(plus_up, passed_up), -1, "output_far")
+    relayed_low = from_y(add(minus_low, passed_low), 1, "output_far")
+    up = add(own_up, got_up, relayed_up).reshape(branches // 2, steps, width)
+    low = add(own_low, got_low, relayed_low).reshape(branches // 2, steps, width)
+    return jnp.concatenate([up, low], axis=0)
 
 
 def solution(mesh):

time: 146 us -> 141 us (0.966)
  waiting for transfers between devices: 52 us -> 44.5 us
  starting transfers between devices: 32.3 us -> 37.2 us
  Pallas kernels: 43.1 us -> 40.7 us
    ppermute x7, waiting for transfers between devices: 10.1 us -> 6.78 us  [from_z(): return lax.ppermute(value, 'branch', perm)]
    ppermute x7, starting transfers between devices: 11.4 us -> 14.6 us  [from_z(): return lax.ppermute(value, 'branch', perm)]
    ppermute x6 -> x9, waiting for transfers between devices: 27.1 us -> 24.2 us  [from_y(): return lax.ppermute(value, 'tensor', perm)]
    pallas_call x2 -> x1, Pallas kernels: 6.92 us -> 4.56 us  [mix(): pl.pallas_call(mix_kernel, out_shape=(out,) * (2 * NY), in_specs=[spec(pl...]
    ppermute x6 -> x9, starting transfers between devices: 11.7 us -> 13.4 us  [from_y(): return lax.ppermute(value, 'tensor', perm)]
  transfers between devices with their start and end apart: 25 -> 28, of which waited for: 11 -> 11; matrix products, arithmetic and copies ran while one was open for 4% -> 5% of each run, Pallas kernels for 21% -> 22%
where the time goes in v2:
time: 141 us
  waiting for transfers between devices  44.5 us (32%)
  Pallas kernels  40.7 us (29%)
  starting transfers between devices  37.2 us (26%)
  local copies, waits for them, and re-layouts  13.8 us (10%)
  other arithmetic  4.11 us (3%)
    ppermute x9, waiting for transfers between devices, from_y(): return lax.ppermute(value, 'tensor', perm)  24.2 us
    ppermute x7, starting transfers between devices, from_z(): return lax.ppermute(value, 'branch', perm)  14.6 us
    ppermute x9, starting transfers between devices, from_y(): return lax.ppermute(value, 'tensor', perm)  13.4 us
    ppermute x6, waiting for transfers between devices, from_x(): return lax.ppermute(value, 'branch', perm)  11.7 us
    pallas_call x1, Pallas kernels, score(): pl.pallas_call(functools.partial(score_kernel, count, len(keys)), out_sha...  10.9 us
    unnamed x65, local copies, waits for them, and re-layouts  10.2 us
    ppermute x6, starting transfers between devices, from_x(): return lax.ppermute(value, 'branch', perm)  7.9 us
    ppermute x7, waiting for transfers between devices, from_z(): return lax.ppermute(value, 'branch', perm)  6.78 us
  transfers between devices with their start and end apart: 28, of which 11 were waited for; matrix products, arithmetic and copies ran while one was open for 5% of the time, Pallas kernels for 22%

profile of v2, /device:TPU:2, one launch (start us, length us, event | category | flops | bytes accessed | tf_op | source)
XLA Modules:
  0.0 140.8 jit_solution(7090481632684586589)
XLA Ops:
  0.0 2.6 %export_pages.1.refs_0_ = bf16[1040,128]{1,0:T(8,128)(2,1)} custom-call(s32[8]{0:T(128)} %picks.1, bf16[2,32]{1,0:T(2,128)(2,1)} %bitcast.14, bf16[32,2,64,128]{3,2,1,0:T(8,128)(2,1)} %codes.1), custom_call_target="tpu_custom_call" | custom-call | tf_op jit(solution)/shard_map/export_pages/pallas_call | solution.py:89
  2.6 2.0 %collective-permute-start.3 = (bf16[1040,128]{1,0:T(8,128)(2,1)}, bf16[1040,128]{1,0:T(8,128)(2,1)S(1)}, u32[]{:S(2)}, u32[]{:S(2)}) collective-permute-start(bf16[1040,128]{1,0:T(8,128)(2,1)} %export_pages.1.refs_0_), channel_id=1, source_target_pairs={{0,32},{8,40},{16,48},{24,56},{32,64},{40,72},{48,80},{56,88},{64,... | collective-permute-start | bytes 798728 | tf_op jit(solution)/shard_map/pages1/ppermute | solution.py:41
  4.6 4.0 %collective-permute-start = (bf16[1040,128]{1,0:T(8,128)(2,1)}, bf16[1040,128]{1,0:T(8,128)(2,1)S(1)}, u32[]{:S(2)}, u32[]{:S(2)}) collective-permute-start(bf16[1040,128]{1,0:T(8,128)(2,1)} %export_pages.1.refs_0_), channel_id=1, source_target_pairs={{0,224},{8,232},{16,240},{24,248},{32,0},{40,8},{48,16},{56,24},{6... | collective-permute-start | bytes 798728 | tf_op jit(solution)/shard_map/pages1/ppermute | solution.py:41
  9.8 3.3 %collective-permute-start.8 = (bf16[512,512]{1,0:T(8,128)(2,1)S(1)}, bf16[512,512]{1,0:T(8,128)(2,1)}, u32[]{:S(2)}, u32[]{:S(2)}) collective-permute-start(bf16[512,512]{1,0:T(8,128)(2,1)S(1)} %reshape.50.refs_0_), channel_id=1, source_target_pairs={{0,4},{1,5},{2,6},{3,7},{4,0},{5,1},{6,2},{7,3},{8,12},{9,13},{10,... | collective-permute-start | bytes 1572872 | tf_op jit(solution)/shard_map/hidden/ppermute | solution.py:53
  14.1 1.5 %collective-permute-done.3.refs_7_ = bf16[1040,128]{1,0:T(8,128)(2,1)S(1)} collective-permute-done((bf16[1040,128]{1,0:T(8,128)(2,1)}, bf16[1040,128]{1,0:T(8,128)(2,1)S(1)}, u32[]{:S(2)}, u32[]{:S(2)}) %collective-permute-start.3) | collective-permute-done | bytes 266272 | tf_op jit(solution)/shard_map/pages1/ppermute | solution.py:41
  16.6 3.1 %collective-permute-start.2 = (bf16[1040,128]{1,0:T(8,128)(2,1)S(1)}, bf16[1040,128]{1,0:T(8,128)(2,1)S(1)}, u32[]{:S(2)}, u32[]{:S(2)}) collective-permute-start(bf16[1040,128]{1,0:T(8,128)(2,1)S(1)} %collective-permute-done.refs_1_), channel_id=1, source_target_pairs={{0,224},{8,232},{16,240},{24,248},{32,0},{40,8},{48,16},{56,24},{6... | collective-permute-start | bytes 798728 | tf_op jit(solution)/shard_map/pages2/ppermute | solution.py:41
  20.8 4.3 %collective-permute-done.2.refs_2_ = bf16[1040,128]{1,0:T(8,128)(2,1)S(1)} collective-permute-done((bf16[1040,128]{1,0:T(8,128)(2,1)S(1)}, bf16[1040,128]{1,0:T(8,128)(2,1)S(1)}, u32[]{:S(2)}, u32[]{:S(2)}) %collective-permute-start.2) | collective-permute-done | bytes 266272 | tf_op jit(solution)/shard_map/pages2/ppermute | solution.py:41
  25.1 3.7 %collective-permute-start.4 = (bf16[1040,128]{1,0:T(8,128)(2,1)S(1)}, bf16[1040,128]{1,0:T(8,128)(2,1)S(1)}, u32[]{:S(2)}, u32[]{:S(2)}) collective-permute-start(bf16[1040,128]{1,0:T(8,128)(2,1)S(1)} %collective-permute-done.2.refs_2_), channel_id=1, source_target_pairs={{0,224},{8,232},{16,240},{24,248},{32,0},{40,8},{48,16},{56,24},{6... | collective-permute-start | bytes 798728 | tf_op jit(solution)/shard_map/pages3/ppermute | solution.py:41
  28.8 8.2 %collective-permute-done.7.refs_1_ = bf16[512,512]{1,0:T(8,128)(2,1)} collective-permute-done((bf16[512,512]{1,0:T(8,128)(2,1)S(1)}, bf16[512,512]{1,0:T(8,128)(2,1)}, u32[]{:S(2)}, u32[]{:S(2)}) %collective-permute-start.7) | collective-permute-done | bytes 524320 | tf_op jit(solution)/shard_map/hidden/ppermute | solution.py:53
  38.7 1.7 %collective-permute-start.12 = (bf16[1040,128]{1,0:T(8,128)(2,1)S(1)}, bf16[1040,128]{1,0:T(8,128)(2,1)S(1)}, u32[]{:S(2)}, u32[]{:S(2)}) collective-permute-start(bf16[1040,128]{1,0:T(8,128)(2,1)S(1)} %collective-permute-done.4.refs_3_), channel_id=1, source_target_pairs={{0,224},{8,232},{16,240},{24,248},{32,0},{40,8},{48,16},{56,24},{6... | collective-permute-start | bytes 798728 | tf_op jit(solution)/shard_map/pages4/ppermute | solution.py:41
  41.8 4.1 %plan.1 = (s32[97]{0:T(128)}, s32[97]{0:T(128)}, s32[96]{0:T(128)}, s32[96]{0:T(128)}, s32[96]{0:T(128)}) custom-call(s32[2]{0:T(128)} %pad_add_fusion.1.where, s32[2048]{0:T(1024)} %reshape.49.pull), custom_call_target="tpu_custom_call" | custom-call | tf_op jit(solution)/shard_map/plan/pallas_call | solution.py:459
  47.6 3.4 %pack.2 = (bf16[2112,128]{1,0:T(8,128)(2,1)}, bf16[2112,128]{1,0:T(8,128)(2,1)}, bf16[2112,128]{1,0:T(8,128)(2,1)}) custom-call(s32[97]{0:T(128)} %get-tuple-element.54.rows, s32[97]{0:T(128)} %get-tuple-element.55.marks, bf16[1040,128]{1,0:T(8,128)(2,1)} %export_pages.1.refs_0_, bf16[1040,128]{1,0:T(8,128)(2,1)} %copy-done.3, bf16[1040,128]{1,0:T(8,128)(2,1)} %copy-done.5, ...), custom_call_target="tpu_custom_call" | custom-call | tf_op jit(solution)/shard_map/pack/pallas_call | solution.py:132
  51.0 1.7 %collective-permute-start.17 = (bf16[2112,128]{1,0:T(8,128)(2,1)}, bf16[2112,128]{1,0:T(8,128)(2,1)}, u32[]{:S(2)}, u32[]{:S(2)}) collective-permute-start(bf16[2112,128]{1,0:T(8,128)(2,1)} %get-tuple-element.60), channel_id=1, source_target_pairs={{0,8},{8,16},{16,24},{24,0},{32,40},{40,48},{48,56},{56,32},{64,72... | collective-permute-start | bytes 1622024 | tf_op jit(solution)/shard_map/key_side/ppermute | solution.py:47
  53.3 2.0 %collective-permute-start.16 = (bf16[2112,128]{1,0:T(8,128)(2,1)}, bf16[2112,128]{1,0:T(8,128)(2,1)}, u32[]{:S(2)}, u32[]{:S(2)}) collective-permute-start(bf16[2112,128]{1,0:T(8,128)(2,1)} %get-tuple-element.61), channel_id=1, source_target_pairs={{0,16},{8,24},{16,0},{24,8},{32,48},{40,56},{48,32},{56,40},{64,80... | collective-permute-start | bytes 1622024 | tf_op jit(solution)/shard_map/key_side/ppermute | solution.py:47
  55.3 1.4 %collective-permute-start.15 = (bf16[2112,128]{1,0:T(8,128)(2,1)}, bf16[2112,128]{1,0:T(8,128)(2,1)}, u32[]{:S(2)}, u32[]{:S(2)}) collective-permute-start(bf16[2112,128]{1,0:T(8,128)(2,1)} %get-tuple-element.62), channel_id=1, source_target_pairs={{0,24},{8,0},{16,8},{24,16},{32,56},{40,32},{48,40},{56,48},{64,88... | collective-permute-start | bytes 1622024 | tf_op jit(solution)/shard_map/key_side/ppermute | solution.py:47
  58.4 3.3 %pack.3 = (bf16[2048,128]{1,0:T(8,128)(2,1)}, bf16[2048,128]{1,0:T(8,128)(2,1)}, bf16[2048,128]{1,0:T(8,128)(2,1)}) custom-call(s32[97]{0:T(128)} %get-tuple-element.54.rows, s32[97]{0:T(128)} %get-tuple-element.55.marks, bf16[1040,128]{1,0:T(8,128)(2,1)} %export_pages.1.refs_0_, bf16[1040,128]{1,0:T(8,128)(2,1)} %copy-done.3, bf16[1040,128]{1,0:T(8,128)(2,1)} %copy-done.5, ...), custom_call_target="tpu_custom_call" | custom-call | tf_op jit(solution)/shard_map/pack/pallas_call | solution.py:132
  61.8 2.2 %copy-done.16 = bf16[4096,512]{1,0:T(8,128)(2,1)S(1)} copy-done((bf16[4096,512]{1,0:T(8,128)(2,1)S(1)}, bf16[4096,512]{1,0:T(8,128)(2,1)}, u32[]{:S(2)}) %copy-start.16) | copy-done | bytes 4194328
  64.0 1.6 %copy-done.17 = bf16[2,4096,128]{2,1,0:T(8,128)(2,1)S(1)} copy-done((bf16[2,4096,128]{2,1,0:T(8,128)(2,1)S(1)}, bf16[2,4096,128]{2,1,0:T(8,128)(2,1)}, u32[]{:S(2)}) %copy-start.17) | copy-done | bytes 2097176
  67.8 6.5 %project.1 = (bf16[2048,128]{1,0:T(8,128)(2,1)S(1)}, bf16[512,128]{1,0:T(8,128)(2,1)S(1)}, bf16[512,128]{1,0:T(8,128)(2,1)S(1)}) custom-call(s32[2]{0:T(128)S(1)} %pad_add_fusion.place, bf16[512,512]{1,0:T(8,128)(2,1)S(1)} %reshape.50.refs_0_, bf16[512,512]{1,0:T(8,128)(2,1)} %collective-permute-done.7.refs_1_, ...), custom_call_target="tpu_custom_call" | custom-call | tf_op jit(solution)/shard_map/project/pallas_call | solution.py:186
  75.7 2.1 %collective-permute-start.18 = (bf16[2048,128]{1,0:T(8,128)(2,1)}, bf16[2048,128]{1,0:T(8,128)(2,1)S(1)}, u32[]{:S(2)}, u32[]{:S(2)}) collective-permute-start(bf16[2048,128]{1,0:T(8,128)(2,1)} %get-tuple-element.71), channel_id=1, source_target_pairs={{0,24},{8,0},{16,8},{24,16},{32,56},{40,32},{48,40},{56,48},{64,88... | collective-permute-start | bytes 1572872 | tf_op jit(solution)/shard_map/value_side/ppermute | solution.py:47
  79.4 2.5 %collective-permute-done.15.refs_8_ = bf16[2112,128]{1,0:T(8,128)(2,1)} collective-permute-done((bf16[2112,128]{1,0:T(8,128)(2,1)}, bf16[2112,128]{1,0:T(8,128)(2,1)}, u32[]{:S(2)}, u32[]{:S(2)}) %collective-permute-start.15) | collective-permute-done | bytes 540704 | tf_op jit(solution)/shard_map/key_side/ppermute | solution.py:47
  83.1 10.9 %score.1 = (bf16[2048,512]{1,0:T(8,128)(2,1)S(1)}, f32[2048,128]{1,0:T(8,128)S(1)}) custom-call(s32[1024]{0:T(1024)S(1)} %reshape.47.table, s32[96]{0:T(128)S(1)} %copy-done.26, s32[96]{0:T(128)S(1)} %copy-done.27, s32[128]{0:T(128)S(1)} %copy-done.24, bf16[2048,128]{1,0:T(8,128)(2,1)S(1)} %copy-done.23, bf16[512,128]{1,0:T(8,128)(2,1)S(1)} %get-tuple-element.66.k_new, ...), custom_call_target="tpu_custom_call" | custom-call | tf_op jit(solution)/shard_map/score/pallas_call | solution.py:307
  94.1 9.1 %collective-permute-done.18.refs_8_ = bf16[2048,128]{1,0:T(8,128)(2,1)S(1)} collective-permute-done((bf16[2048,128]{1,0:T(8,128)(2,1)}, bf16[2048,128]{1,0:T(8,128)(2,1)S(1)}, u32[]{:S(2)}, u32[]{:S(2)}) %collective-permute-start.18) | collective-permute-done | bytes 524320 | tf_op jit(solution)/shard_map/value_side/ppermute | solution.py:47
  103.2 5.3 %value.1.near = bf16[512,512]{1,0:T(8,128)(2,1)S(1)} custom-call(s32[1024]{0:T(1024)S(1)} %reshape.47.table, s32[96]{0:T(128)S(1)} %copy-done.25, bf16[2048,512]{1,0:T(8,128)(2,1)S(1)} %get-tuple-element.68.weights, f32[2048,128]{1,0:T(8,128)S(1)} %get-tuple-element.69.fresh, bf16[1040,128]{1,0:T(8,128)(2,1)S(1)} %copy-done, ...), custom_call_target="tpu_custom_call" | custom-call | tf_op jit(solution)/shard_map/value/pallas_call | solution.py:354
  108.8 1.9 %collective-permute-done.21.far = bf16[512,512]{1,0:T(8,128)(2,1)S(1)} collective-permute-done((bf16[512,512]{1,0:T(8,128)(2,1)S(1)}, bf16[512,512]{1,0:T(8,128)(2,1)S(1)}, u32[]{:S(2)}, u32[]{:S(2)}) %collective-permute-start.21) | collective-permute-done | bytes 524320 | tf_op jit(solution)/shard_map/attended_core/ppermute | solution.py:58
  110.7 4.6 %mix.1 = (bf16[256,512]{1,0:T(8,128)(2,1)S(1)}, bf16[256,512]{1,0:T(8,128)(2,1)S(1)}, bf16[256,512]{1,0:T(8,128)(2,1)S(1)}, bf16[256,512]{1,0:T(8,128)(2,1)S(1)}...) custom-call(s32[2]{0:T(128)S(1)} %pad_add_fusion.place, ...), custom_call_target="tpu_custom_call" | custom-call | tf_op jit(solution)/shard_map/mix/pallas_call | solution.py:389
  115.6 3.0 %collective-permute-start.26 = (bf16[256,512]{1,0:T(8,128)(2,1)S(1)}, bf16[256,512]{1,0:T(8,128)(2,1)S(1)}, u32[]{:S(2)}, u32[]{:S(2)}) collective-permute-start(bf16[256,512]{1,0:T(8,128)(2,1)S(1)} %get-tuple-element.82), channel_id=1, source_target_pairs={{0,6},{1,7},{2,0},{3,1},{4,2},{5,3},{6,4},{7,5},{8,14},{9,15},{10,... | collective-permute-start | bytes 786440 | tf_op jit(solution)/shard_map/output_relay/ppermute | solution.py:53
  119.1 5.9 %collective-permute-done.23 = bf16[256,512]{1,0:T(8,128)(2,1)S(1)} collective-permute-done((bf16[256,512]{1,0:T(8,128)(2,1)S(1)}, bf16[256,512]{1,0:T(8,128)(2,1)S(1)}, u32[]{:S(2)}, u32[]{:S(2)}) %collective-permute-start.23) | collective-permute-done | bytes 262176 | tf_op jit(solution)/shard_map/output_relay/ppermute | solution.py:53
  126.1 3.0 %collective-permute-start.27 = (bf16[256,512]{1,0:T(8,128)(2,1)S(1)}, bf16[256,512]{1,0:T(8,128)(2,1)S(1)}, u32[]{:S(2)}, u32[]{:S(2)}) collective-permute-start(bf16[256,512]{1,0:T(8,128)(2,1)S(1)} %add_convert_fusion.1), channel_id=1, source_target_pairs={{0,6},{1,7},{2,0},{3,1},{4,2},{5,3},{6,4},{7,5},{8,14},{9,15},{10,... | collective-permute-start | bytes 786440 | tf_op jit(solution)/shard_map/output_far/ppermute | solution.py:53
  129.2 1.8 %collective-permute-done.22 = bf16[256,512]{1,0:T(8,128)(2,1)S(1)} collective-permute-done((bf16[256,512]{1,0:T(8,128)(2,1)S(1)}, bf16[256,512]{1,0:T(8,128)(2,1)S(1)}, u32[]{:S(2)}, u32[]{:S(2)}) %collective-permute-start.22) | collective-permute-done | bytes 262176 | tf_op jit(solution)/shard_map/output_near/ppermute | solution.py:53
  130.9 4.6 %collective-permute-done.24 = bf16[256,512]{1,0:T(8,128)(2,1)S(1)} collective-permute-done((bf16[256,512]{1,0:T(8,128)(2,1)S(1)}, bf16[256,512]{1,0:T(8,128)(2,1)S(1)}, u32[]{:S(2)}, u32[]{:S(2)}) %collective-permute-start.24) | collective-permute-done | bytes 262176 | tf_op jit(solution)/shard_map/output_far/ppermute | solution.py:53
  135.7 3.7 %collective-permute-done.25 = bf16[256,512]{1,0:T(8,128)(2,1)S(1)} collective-permute-done((bf16[256,512]{1,0:T(8,128)(2,1)S(1)}, bf16[256,512]{1,0:T(8,128)(2,1)S(1)}, u32[]{:S(2)}, u32[]{:S(2)}) %collective-permute-start.25) | collective-permute-done | bytes 262176 | tf_op jit(solution)/shard_map/output_near/ppermute | solution.py:53
  (118 shorter events, 21.2 us)
Async XLA Ops:
  0.0 40.5 %copy-start.28 = (s32[32,64]{1,0:T(8,128)S(1)}, s32[32,64]{1,0:T(8,128)}, u32[]{:S(2)}) copy-start(s32[32,64]{1,0:T(8,128)} %param.19) | copy-start | bytes 24580
  0.0 56.8 %copy-start.29 = (f32[4096]{0:T(1024)S(1)}, f32[4096]{0:T(1024)}, u32[]{:S(2)}) copy-start(f32[4096]{0:T(1024)} %param.12) | copy-start | bytes 49156
  0.0 16.5 %collective-permute-start.1 = (bf16[512,4096]{1,0:T(8,128)(2,1)}, bf16[512,4096]{1,0:T(8,128)(2,1)}, u32[]{:S(2)}, u32[]{:S(2)}) collective-permute-start(bf16[512,4096]{1,0:T(8,128)(2,1)} %w_near.1), channel_id=1, source_target_pairs={{0,1},{1,0},{2,3},{3,2},{4,5},{5,4},{6,7},{7,6},{8,9},{9,8},{10,11... | collective-permute-start | bytes 12582920 | tf_op jit(solution)/shard_map/w_out/ppermute | solution.py:58
  2.6 13.1 %collective-permute-start.3 = (bf16[1040,128]{1,0:T(8,128)(2,1)}, bf16[1040,128]{1,0:T(8,128)(2,1)S(1)}, u32[]{:S(2)}, u32[]{:S(2)}) collective-permute-start(bf16[1040,128]{1,0:T(8,128)(2,1)} %export_pages.1.refs_0_), channel_id=1, source_target_pairs={{0,32},{8,40},{16,48},{24,56},{32,64},{40,72},{48,80},{56,88},{64,... | collective-permute-start | bytes 798728 | tf_op jit(solution)/shard_map/pages1/ppermute | solution.py:41
  4.6 11.1 %collective-permute-start = (bf16[1040,128]{1,0:T(8,128)(2,1)}, bf16[1040,128]{1,0:T(8,128)(2,1)S(1)}, u32[]{:S(2)}, u32[]{:S(2)}) collective-permute-start(bf16[1040,128]{1,0:T(8,128)(2,1)} %export_pages.1.refs_0_), channel_id=1, source_target_pairs={{0,224},{8,232},{16,240},{24,248},{32,0},{40,8},{48,16},{56,24},{6... | collective-permute-start | bytes 798728 | tf_op jit(solution)/shard_map/pages1/ppermute | solution.py:41
  9.8 19.0 %collective-permute-start.8 = (bf16[512,512]{1,0:T(8,128)(2,1)S(1)}, bf16[512,512]{1,0:T(8,128)(2,1)}, u32[]{:S(2)}, u32[]{:S(2)}) collective-permute-start(bf16[512,512]{1,0:T(8,128)(2,1)S(1)} %reshape.50.refs_0_), channel_id=1, source_target_pairs={{0,4},{1,5},{2,6},{3,7},{4,0},{5,1},{6,2},{7,3},{8,12},{9,13},{10,... | collective-permute-start | bytes 1572872 | tf_op jit(solution)/shard_map/hidden/ppermute | solution.py:53
  13.1 23.9 %collective-permute-start.7 = (bf16[512,512]{1,0:T(8,128)(2,1)S(1)}, bf16[512,512]{1,0:T(8,128)(2,1)}, u32[]{:S(2)}, u32[]{:S(2)}) collective-permute-start(bf16[512,512]{1,0:T(8,128)(2,1)S(1)} %reshape.50.refs_0_), channel_id=1, source_target_pairs={{0,6},{1,7},{2,0},{3,1},{4,2},{5,3},{6,4},{7,5},{8,14},{9,15},{10,... | collective-permute-start | bytes 1572872 | tf_op jit(solution)/shard_map/hidden/ppermute | solution.py:53
  15.7 31.2 %copy-start.1 = (bf16[1040,128]{1,0:T(8,128)(2,1)}, bf16[1040,128]{1,0:T(8,128)(2,1)S(1)}, u32[]{:S(2)}) copy-start(bf16[1040,128]{1,0:T(8,128)(2,1)S(1)} %collective-permute-done.3.refs_7_) | copy-start | bytes 798724
  15.7 31.2 %copy-start.3 = (bf16[1040,128]{1,0:T(8,128)(2,1)}, bf16[1040,128]{1,0:T(8,128)(2,1)S(1)}, u32[]{:S(2)}) copy-start(bf16[1040,128]{1,0:T(8,128)(2,1)S(1)} %collective-permute-done.refs_1_) | copy-start | bytes 798724
  16.6 8.6 %collective-permute-start.2 = (bf16[1040,128]{1,0:T(8,128)(2,1)S(1)}, bf16[1040,128]{1,0:T(8,128)(2,1)S(1)}, u32[]{:S(2)}, u32[]{:S(2)}) collective-permute-start(bf16[1040,128]{1,0:T(8,128)(2,1)S(1)} %collective-permute-done.refs_1_), channel_id=1, source_target_pairs={{0,224},{8,232},{16,240},{24,248},{32,0},{40,8},{48,16},{56,24},{6... | collective-permute-start | bytes 798728 | tf_op jit(solution)/shard_map/pages2/ppermute | solution.py:41
  19.6 9.2 %collective-permute-start.5 = (bf16[1040,128]{1,0:T(8,128)(2,1)S(1)}, bf16[1040,128]{1,0:T(8,128)(2,1)S(1)}, u32[]{:S(2)}, u32[]{:S(2)}) collective-permute-start(bf16[1040,128]{1,0:T(8,128)(2,1)S(1)} %collective-permute-done.3.refs_7_), channel_id=1, source_target_pairs={{0,32},{8,40},{16,48},{24,56},{32,64},{40,72},{48,80},{56,88},{64,... | collective-permute-start | bytes 798728 | tf_op jit(solution)/shard_map/pages2/ppermute | solution.py:41
  25.1 13.6 %collective-permute-start.4 = (bf16[1040,128]{1,0:T(8,128)(2,1)S(1)}, bf16[1040,128]{1,0:T(8,128)(2,1)S(1)}, u32[]{:S(2)}, u32[]{:S(2)}) collective-permute-start(bf16[1040,128]{1,0:T(8,128)(2,1)S(1)} %collective-permute-done.2.refs_2_), channel_id=1, source_target_pairs={{0,224},{8,232},{16,240},{24,248},{32,0},{40,8},{48,16},{56,24},{6... | collective-permute-start | bytes 798728 | tf_op jit(solution)/shard_map/pages3/ppermute | solution.py:41
  28.8 9.9 %collective-permute-start.6 = (bf16[1040,128]{1,0:T(8,128)(2,1)S(1)}, bf16[1040,128]{1,0:T(8,128)(2,1)S(1)}, u32[]{:S(2)}, u32[]{:S(2)}) collective-permute-start(bf16[1040,128]{1,0:T(8,128)(2,1)S(1)} %collective-permute-done.5.refs_6_), channel_id=1, source_target_pairs={{0,32},{8,40},{16,48},{24,56},{32,64},{40,72},{48,80},{56,88},{64,... | collective-permute-start | bytes 798728 | tf_op jit(solution)/shard_map/pages3/ppermute | solution.py:41
  37.0 8.8 %collective-permute-start.10 = (bf16[512,512]{1,0:T(8,128)(2,1)}, bf16[512,512]{1,0:T(8,128)(2,1)}, u32[]{:S(2)}, u32[]{:S(2)}) collective-permute-start(bf16[512,512]{1,0:T(8,128)(2,1)} %collective-permute-done.7.refs_1_), channel_id=1, source_target_pairs={{0,1},{1,0},{2,3},{3,2},{4,5},{5,4},{6,7},{7,6},{8,9},{9,8},{10,11... | collective-permute-start | bytes 1572872 | tf_op jit(solution)/shard_map/hidden_core/ppermute | solution.py:58
  37.0 8.8 %collective-permute-start.11 = (bf16[512,512]{1,0:T(8,128)(2,1)}, bf16[512,512]{1,0:T(8,128)(2,1)}, u32[]{:S(2)}, u32[]{:S(2)}) collective-permute-start(bf16[512,512]{1,0:T(8,128)(2,1)} %collective-permute-done.8.refs_2_), channel_id=1, source_target_pairs={{0,1},{1,0},{2,3},{3,2},{4,5},{5,4},{6,7},{7,6},{8,9},{9,8},{10,11... | collective-permute-start | bytes 1572872 | tf_op jit(solution)/shard_map/hidden_core/ppermute | solution.py:58
  37.5 15.2 %collective-permute-start.9 = (bf16[512,512]{1,0:T(8,128)(2,1)S(1)}, bf16[512,512]{1,0:T(8,128)(2,1)}, u32[]{:S(2)}, u32[]{:S(2)}) collective-permute-start(bf16[512,512]{1,0:T(8,128)(2,1)S(1)} %reshape.50.refs_0_), channel_id=1, source_target_pairs={{0,2},{1,3},{2,4},{3,5},{4,6},{5,7},{6,0},{7,1},{8,10},{9,11},{10,... | collective-permute-start | bytes 1572872 | tf_op jit(solution)/shard_map/hidden/ppermute | solution.py:53
  38.7 8.1 %collective-permute-start.12 = (bf16[1040,128]{1,0:T(8,128)(2,1)S(1)}, bf16[1040,128]{1,0:T(8,128)(2,1)S(1)}, u32[]{:S(2)}, u32[]{:S(2)}) collective-permute-start(bf16[1040,128]{1,0:T(8,128)(2,1)S(1)} %collective-permute-done.4.refs_3_), channel_id=1, source_target_pairs={{0,224},{8,232},{16,240},{24,248},{32,0},{40,8},{48,16},{56,24},{6... | collective-permute-start | bytes 798728 | tf_op jit(solution)/shard_map/pages4/ppermute | solution.py:41
  51.0 26.7 %collective-permute-start.17 = (bf16[2112,128]{1,0:T(8,128)(2,1)}, bf16[2112,128]{1,0:T(8,128)(2,1)}, u32[]{:S(2)}, u32[]{:S(2)}) collective-permute-start(bf16[2112,128]{1,0:T(8,128)(2,1)} %get-tuple-element.60), channel_id=1, source_target_pairs={{0,8},{8,16},{16,24},{24,0},{32,40},{40,48},{48,56},{56,32},{64,72... | collective-permute-start | bytes 1622024 | tf_op jit(solution)/shard_map/key_side/ppermute | solution.py:47
  52.7 4.1 %collective-permute-start.13 = (bf16[512,512]{1,0:T(8,128)(2,1)S(1)}, bf16[512,512]{1,0:T(8,128)(2,1)S(1)}, u32[]{:S(2)}, u32[]{:S(2)}) collective-permute-start(bf16[512,512]{1,0:T(8,128)(2,1)S(1)} %reshape.50.refs_0_), channel_id=1, source_target_pairs={{0,1},{1,0},{2,3},{3,2},{4,5},{5,4},{6,7},{7,6},{8,9},{9,8},{10,11... | collective-permute-start | bytes 1572872 | tf_op jit(solution)/shard_map/hidden_core/ppermute | solution.py:58
  52.8 4.9 %collective-permute-start.14 = (bf16[512,512]{1,0:T(8,128)(2,1)}, bf16[512,512]{1,0:T(8,128)(2,1)S(1)}, u32[]{:S(2)}, u32[]{:S(2)}) collective-permute-start(bf16[512,512]{1,0:T(8,128)(2,1)} %collective-permute-done.9.refs_3_), channel_id=1, source_target_pairs={{0,1},{1,0},{2,3},{3,2},{4,5},{5,4},{6,7},{7,6},{8,9},{9,8},{10,11... | collective-permute-start | bytes 1572872 | tf_op jit(solution)/shard_map/hidden_core/ppermute | solution.py:58
  53.3 26.1 %collective-permute-start.16 = (bf16[2112,128]{1,0:T(8,128)(2,1)}, bf16[2112,128]{1,0:T(8,128)(2,1)}, u32[]{:S(2)}, u32[]{:S(2)}) collective-permute-start(bf16[2112,128]{1,0:T(8,128)(2,1)} %get-tuple-element.61), channel_id=1, source_target_pairs={{0,16},{8,24},{16,0},{24,8},{32,48},{40,56},{48,32},{56,40},{64,80... | collective-permute-start | bytes 1622024 | tf_op jit(solution)/shard_map/key_side/ppermute | solution.py:47
  55.3 26.6 %collective-permute-start.15 = (bf16[2112,128]{1,0:T(8,128)(2,1)}, bf16[2112,128]{1,0:T(8,128)(2,1)}, u32[]{:S(2)}, u32[]{:S(2)}) collective-permute-start(bf16[2112,128]{1,0:T(8,128)(2,1)} %get-tuple-element.62), channel_id=1, source_target_pairs={{0,24},{8,0},{16,8},{24,16},{32,56},{40,32},{48,40},{56,48},{64,88... | collective-permute-start | bytes 1622024 | tf_op jit(solution)/shard_map/key_side/ppermute | solution.py:47
  75.1 19.0 %collective-permute-start.19 = (bf16[2048,128]{1,0:T(8,128)(2,1)}, bf16[2048,128]{1,0:T(8,128)(2,1)S(1)}, u32[]{:S(2)}, u32[]{:S(2)}) collective-permute-start(bf16[2048,128]{1,0:T(8,128)(2,1)} %get-tuple-element.73), channel_id=1, source_target_pairs={{0,16},{8,24},{16,0},{24,8},{32,48},{40,56},{48,32},{56,40},{64,80... | collective-permute-start | bytes 1572872 | tf_op jit(solution)/shard_map/value_side/ppermute | solution.py:47
  75.7 27.5 %collective-permute-start.18 = (bf16[2048,128]{1,0:T(8,128)(2,1)}, bf16[2048,128]{1,0:T(8,128)(2,1)S(1)}, u32[]{:S(2)}, u32[]{:S(2)}) collective-permute-start(bf16[2048,128]{1,0:T(8,128)(2,1)} %get-tuple-element.71), channel_id=1, source_target_pairs={{0,24},{8,0},{16,8},{24,16},{32,56},{40,32},{48,40},{56,48},{64,88... | collective-permute-start | bytes 1572872 | tf_op jit(solution)/shard_map/value_side/ppermute | solution.py:47
  77.8 25.5 %collective-permute-start.20 = (bf16[2048,128]{1,0:T(8,128)(2,1)}, bf16[2048,128]{1,0:T(8,128)(2,1)}, u32[]{:S(2)}, u32[]{:S(2)}) collective-permute-start(bf16[2048,128]{1,0:T(8,128)(2,1)} %get-tuple-element.74), channel_id=1, source_target_pairs={{0,8},{8,16},{16,24},{24,0},{32,40},{40,48},{48,56},{56,32},{64,72... | collective-permute-start | bytes 1572872 | tf_op jit(solution)/shard_map/value_side/ppermute | solution.py:47
  108.5 2.2 %collective-permute-start.21 = (bf16[512,512]{1,0:T(8,128)(2,1)S(1)}, bf16[512,512]{1,0:T(8,128)(2,1)S(1)}, u32[]{:S(2)}, u32[]{:S(2)}) collective-permute-start(bf16[512,512]{1,0:T(8,128)(2,1)S(1)} %value.1.near), channel_id=1, source_target_pairs={{0,1},{1,0},{2,3},{3,2},{4,5},{5,4},{6,7},{7,6},{8,9},{9,8},{10,11... | collective-permute-start | bytes 1572872 | tf_op jit(solution)/shard_map/attended_core/ppermute | solution.py:58
  115.3 9.6 %collective-permute-start.23 = (bf16[256,512]{1,0:T(8,128)(2,1)S(1)}, bf16[256,512]{1,0:T(8,128)(2,1)S(1)}, u32[]{:S(2)}, u32[]{:S(2)}) collective-permute-start(bf16[256,512]{1,0:T(8,128)(2,1)S(1)} %get-tuple-element.78), channel_id=1, source_target_pairs={{0,2},{1,3},{2,4},{3,5},{4,6},{5,7},{6,0},{7,1},{8,10},{9,11},{10,... | collective-permute-start | bytes 786440 | tf_op jit(solution)/shard_map/output_relay/ppermute | solution.py:53
  115.6 10.4 %collective-permute-start.26 = (bf16[256,512]{1,0:T(8,128)(2,1)S(1)}, bf16[256,512]{1,0:T(8,128)(2,1)S(1)}, u32[]{:S(2)}, u32[]{:S(2)}) collective-permute-start(bf16[256,512]{1,0:T(8,128)(2,1)S(1)} %get-tuple-element.82), channel_id=1, source_target_pairs={{0,6},{1,7},{2,0},{3,1},{4,2},{5,3},{6,4},{7,5},{8,14},{9,15},{10,... | collective-permute-start | bytes 786440 | tf_op jit(solution)/shard_map/output_relay/ppermute | solution.py:53
  118.6 12.3 %collective-permute-start.22 = (bf16[256,512]{1,0:T(8,128)(2,1)S(1)}, bf16[256,512]{1,0:T(8,128)(2,1)S(1)}, u32[]{:S(2)}, u32[]{:S(2)}) collective-permute-start(bf16[256,512]{1,0:T(8,128)(2,1)S(1)} %get-tuple-element.76), channel_id=1, source_target_pairs={{0,6},{1,7},{2,0},{3,1},{4,2},{5,3},{6,4},{7,5},{8,14},{9,15},{10,... | collective-permute-start | bytes 786440 | tf_op jit(solution)/shard_map/output_near/ppermute | solution.py:53
  125.0 10.5 %collective-permute-start.24 = (bf16[256,512]{1,0:T(8,128)(2,1)S(1)}, bf16[256,512]{1,0:T(8,128)(2,1)S(1)}, u32[]{:S(2)}, u32[]{:S(2)}) collective-permute-start(bf16[256,512]{1,0:T(8,128)(2,1)S(1)} %add_convert_fusion.3), channel_id=1, source_target_pairs={{0,2},{1,3},{2,4},{3,5},{4,6},{5,7},{6,0},{7,1},{8,10},{9,11},{10,... | collective-permute-start | bytes 786440 | tf_op jit(solution)/shard_map/output_far/ppermute | solution.py:53
  125.1 14.3 %collective-permute-start.25 = (bf16[256,512]{1,0:T(8,128)(2,1)S(1)}, bf16[256,512]{1,0:T(8,128)(2,1)S(1)}, u32[]{:S(2)}, u32[]{:S(2)}) collective-permute-start(bf16[256,512]{1,0:T(8,128)(2,1)S(1)} %get-tuple-element.80), channel_id=1, source_target_pairs={{0,2},{1,3},{2,4},{3,5},{4,6},{5,7},{6,0},{7,1},{8,10},{9,11},{10,... | collective-permute-start | bytes 786440 | tf_op jit(solution)/shard_map/output_near/ppermute | solution.py:53
  126.1 13.3 %collective-permute-start.27 = (bf16[256,512]{1,0:T(8,128)(2,1)S(1)}, bf16[256,512]{1,0:T(8,128)(2,1)S(1)}, u32[]{:S(2)}, u32[]{:S(2)}) collective-permute-start(bf16[256,512]{1,0:T(8,128)(2,1)S(1)} %add_convert_fusion.1), channel_id=1, source_target_pairs={{0,6},{1,7},{2,0},{3,1},{4,2},{5,3},{6,4},{7,5},{8,14},{9,15},{10,... | collective-permute-start | bytes 786440 | tf_op jit(solution)/shard_map/output_far/ppermute | solution.py:53
  (28 other events, 289.0 us)

commit v3 on v2

--- a/solution.py
+++ b/solution.py
@@ -372,25 +372,25 @@
     )(table, vrow, weights, fresh, *values)
 
 
-def mix_kernel(place, near, far, w_near, w_far, *outs):
+def mix_kernel(blocks, place, near, far, w_near, w_far, *outs):
     y, c = place[0], place[1]
     half, width = outs[0].shape
-    for j in (2, 1, 3, 0):
+    for i, j in enumerate(blocks):
         at = pl.ds(pl.multiple_of((lax.rem(y + j, NY) * 2 + c) * width, width), width)
         total = jnp.dot(near[...], w_near[:, at], preferred_element_type=jnp.float32)
         total += jnp.dot(far[...], w_far[:, at], preferred_element_type=jnp.float32)
-        outs[2 * j][...] = total[:half].astype(jnp.bfloat16)
-        outs[2 * j + 1][...] = total[half:].astype(jnp.bfloat16)
-
-
-def mix(place, near, far, w_near, w_far):
+        outs[2 * i][...] = total[:half].astype(jnp.bfloat16)
+        outs[2 * i + 1][...] = total[half:].astype(jnp.bfloat16)
+
+
+def mix(blocks, place, near, far, w_near, w_far):
     width = w_near.shape[1] // (2 * NY)
     out = jax.ShapeDtypeStruct((near.shape[0] // 2, width), jnp.bfloat16)
     return pl.pallas_call(
-        mix_kernel,
-        out_shape=(out,) * (2 * NY),
+        functools.partial(mix_kernel, blocks),
+        out_shape=(out,) * (2 * len(blocks)),
         in_specs=[spec(pltpu.SMEM)] + [spec(pltpu.VMEM)] * 4,
-        out_specs=(spec(pltpu.VMEM),) * (2 * NY),
+        out_specs=(spec(pltpu.VMEM),) * (2 * len(blocks)),
         compiler_params=pltpu.CompilerParams(vmem_limit_bytes=LIMIT),
         name="mix",
     )(place, near, far, w_near, w_far)
@@ -537,8 +537,12 @@
     weights, fresh = score(table, krow, mark, lengths, q, k_new, v_new, own_scales, keys)
     attended = value(0, branches, table, vrow, weights, fresh, values)
     other = from_core(attended, "attended_core")
-    own_up, own_low, plus_up, plus_low, across_up, across_low, minus_up, minus_low = mix(
-        place, attended, other, w_out, w_far
+    across_up, across_low = mix((2,), place, attended, other, w_out, w_far)
+    passed_up = from_y(across_up, -1, "output_relay")
+    passed_low = from_y(across_low, 1, "output_relay")
+    attended = after(attended, across_up)
+    plus_up, plus_low, minus_up, minus_low, own_up, own_low = mix(
+        (1, 3, 0), place, attended, other, w_out, w_far
     )
 
     def add(*terms):
@@ -547,8 +551,6 @@
             total = total + term.astype(jnp.float32)
         return total.astype(jnp.bfloat16)
 
-    passed_up = from_y(across_up, -1, "output_relay")
-    passed_low = from_y(across_low, 1, "output_relay")
     got_low = from_y(plus_low, -1, "output_near")
     got_up = from_y(minus_up, 1, "output_near")
     relayed_up = from_y(add(plus_up, passed_up), -1, "output_far")

time: 141 us -> 139 us (0.986); the launches traced: 141 us -> 137 us
  waiting for transfers between devices: 44.5 us -> 39.7 us
  Pallas kernels: 40.7 us -> 43 us
    ppermute x9, waiting for transfers between devices: 24.2 us -> 19.2 us  [from_y(): return lax.ppermute(value, 'tensor', perm)]
    pallas_call x1 -> x2, Pallas kernels: 4.56 us -> 6.91 us  [mix(): pl.pallas_call(functools.partial(mix_kernel, blocks), out_shape=(out,) *...]
  transfers between devices with their start and end apart: 28 -> 28, of which waited for: 11 -> 13; matrix products, arithmetic and copies ran while one was open for 5% -> 5% of each run, Pallas kernels for 22% -> 25%
where the time goes in v3:
time: 139 us; the launch traced here: 137 us
  Pallas kernels  43 us (31%)
  waiting for transfers between devices  39.7 us (29%)
  starting transfers between devices  36.3 us (26%)
  local copies, waits for them, and re-layouts  13.8 us (10%)
  other arithmetic  4.06 us (3%)
    ppermute x9, waiting for transfers between devices, from_y(): return lax.ppermute(value, 'tensor', perm)  19.2 us
    ppermute x7, starting transfers between devices, from_z(): return lax.ppermute(value, 'branch', perm)  14.6 us
    ppermute x9, starting transfers between devices, from_y(): return lax.ppermute(value, 'tensor', perm)  12.7 us
    ppermute x6, waiting for transfers between devices, from_x(): return lax.ppermute(value, 'branch', perm)  11.7 us
    pallas_call x1, Pallas kernels, score(): pl.pallas_call(functools.partial(score_kernel, count, len(keys)), out_sha...  10.9 us
    unnamed x65, local copies, waits for them, and re-layouts  10.1 us
    ppermute x6, starting transfers between devices, from_x(): return lax.ppermute(value, 'branch', perm)  7.91 us
    pallas_call x2, Pallas kernels, mix(): pl.pallas_call(functools.partial(mix_kernel, blocks), out_shape=(out,) *...  6.91 us
  transfers between devices with their start and end apart: 28, of which 13 were waited for; matrix products, arithmetic and copies ran while one was open for 5% of the time, Pallas kernels for 25%

profile of v3, /device:TPU:2, one launch (start us, length us, event | category | flops | bytes accessed | tf_op | source)
XLA Modules:
  0.0 137.2 jit_solution(17960106914907906924)
XLA Ops:
  0.0 2.5 %export_pages.1.refs_0_ = bf16[1040,128]{1,0:T(8,128)(2,1)} custom-call(s32[8]{0:T(128)} %picks.1, bf16[2,32]{1,0:T(2,128)(2,1)} %bitcast.14, bf16[32,2,64,128]{3,2,1,0:T(8,128)(2,1)} %codes.1), custom_call_target="tpu_custom_call" | custom-call | tf_op jit(solution)/shard_map/export_pages/pallas_call | solution.py:89
  2.6 2.0 %collective-permute-start.3 = (bf16[1040,128]{1,0:T(8,128)(2,1)}, bf16[1040,128]{1,0:T(8,128)(2,1)S(1)}, u32[]{:S(2)}, u32[]{:S(2)}) collective-permute-start(bf16[1040,128]{1,0:T(8,128)(2,1)} %export_pages.1.refs_0_), channel_id=1, source_target_pairs={{0,32},{8,40},{16,48},{24,56},{32,64},{40,72},{48,80},{56,88},{64,... | collective-permute-start | bytes 798728 | tf_op jit(solution)/shard_map/pages1/ppermute | solution.py:41
  4.6 4.0 %collective-permute-start = (bf16[1040,128]{1,0:T(8,128)(2,1)}, bf16[1040,128]{1,0:T(8,128)(2,1)S(1)}, u32[]{:S(2)}, u32[]{:S(2)}) collective-permute-start(bf16[1040,128]{1,0:T(8,128)(2,1)} %export_pages.1.refs_0_), channel_id=1, source_target_pairs={{0,224},{8,232},{16,240},{24,248},{32,0},{40,8},{48,16},{56,24},{6... | collective-permute-start | bytes 798728 | tf_op jit(solution)/shard_map/pages1/ppermute | solution.py:41
  9.8 3.3 %collective-permute-start.8 = (bf16[512,512]{1,0:T(8,128)(2,1)S(1)}, bf16[512,512]{1,0:T(8,128)(2,1)}, u32[]{:S(2)}, u32[]{:S(2)}) collective-permute-start(bf16[512,512]{1,0:T(8,128)(2,1)S(1)} %reshape.50.refs_0_), channel_id=1, source_target_pairs={{0,4},{1,5},{2,6},{3,7},{4,0},{5,1},{6,2},{7,3},{8,12},{9,13},{10,... | collective-permute-start | bytes 1572872 | tf_op jit(solution)/shard_map/hidden/ppermute | solution.py:53
  14.1 1.5 %collective-permute-done.3.refs_7_ = bf16[1040,128]{1,0:T(8,128)(2,1)S(1)} collective-permute-done((bf16[1040,128]{1,0:T(8,128)(2,1)}, bf16[1040,128]{1,0:T(8,128)(2,1)S(1)}, u32[]{:S(2)}, u32[]{:S(2)}) %collective-permute-start.3) | collective-permute-done | bytes 266272 | tf_op jit(solution)/shard_map/pages1/ppermute | solution.py:41
  16.5 3.1 %collective-permute-start.2 = (bf16[1040,128]{1,0:T(8,128)(2,1)S(1)}, bf16[1040,128]{1,0:T(8,128)(2,1)S(1)}, u32[]{:S(2)}, u32[]{:S(2)}) collective-permute-start(bf16[1040,128]{1,0:T(8,128)(2,1)S(1)} %collective-permute-done.refs_1_), channel_id=1, source_target_pairs={{0,224},{8,232},{16,240},{24,248},{32,0},{40,8},{48,16},{56,24},{6... | collective-permute-start | bytes 798728 | tf_op jit(solution)/shard_map/pages2/ppermute | solution.py:41
  20.8 4.3 %collective-permute-done.2.refs_2_ = bf16[1040,128]{1,0:T(8,128)(2,1)S(1)} collective-permute-done((bf16[1040,128]{1,0:T(8,128)(2,1)S(1)}, bf16[1040,128]{1,0:T(8,128)(2,1)S(1)}, u32[]{:S(2)}, u32[]{:S(2)}) %collective-permute-start.2) | collective-permute-done | bytes 266272 | tf_op jit(solution)/shard_map/pages2/ppermute | solution.py:41
  25.1 3.7 %collective-permute-start.4 = (bf16[1040,128]{1,0:T(8,128)(2,1)S(1)}, bf16[1040,128]{1,0:T(8,128)(2,1)S(1)}, u32[]{:S(2)}, u32[]{:S(2)}) collective-permute-start(bf16[1040,128]{1,0:T(8,128)(2,1)S(1)} %collective-permute-done.2.refs_2_), channel_id=1, source_target_pairs={{0,224},{8,232},{16,240},{24,248},{32,0},{40,8},{48,16},{56,24},{6... | collective-permute-start | bytes 798728 | tf_op jit(solution)/shard_map/pages3/ppermute | solution.py:41
  28.8 8.2 %collective-permute-done.7.refs_1_ = bf16[512,512]{1,0:T(8,128)(2,1)} collective-permute-done((bf16[512,512]{1,0:T(8,128)(2,1)S(1)}, bf16[512,512]{1,0:T(8,128)(2,1)}, u32[]{:S(2)}, u32[]{:S(2)}) %collective-permute-start.7) | collective-permute-done | bytes 524320 | tf_op jit(solution)/shard_map/hidden/ppermute | solution.py:53
  38.7 1.7 %collective-permute-start.12 = (bf16[1040,128]{1,0:T(8,128)(2,1)S(1)}, bf16[1040,128]{1,0:T(8,128)(2,1)S(1)}, u32[]{:S(2)}, u32[]{:S(2)}) collective-permute-start(bf16[1040,128]{1,0:T(8,128)(2,1)S(1)} %collective-permute-done.4.refs_3_), channel_id=1, source_target_pairs={{0,224},{8,232},{16,240},{24,248},{32,0},{40,8},{48,16},{56,24},{6... | collective-permute-start | bytes 798728 | tf_op jit(solution)/shard_map/pages4/ppermute | solution.py:41
  41.7 4.1 %plan.1 = (s32[97]{0:T(128)}, s32[97]{0:T(128)}, s32[96]{0:T(128)}, s32[96]{0:T(128)}, s32[96]{0:T(128)}) custom-call(s32[2]{0:T(128)} %pad_add_fusion.1.where, s32[2048]{0:T(1024)} %reshape.49.pull), custom_call_target="tpu_custom_call" | custom-call | tf_op jit(solution)/shard_map/plan/pallas_call | solution.py:459
  47.5 3.4 %pack.2 = (bf16[2112,128]{1,0:T(8,128)(2,1)}, bf16[2112,128]{1,0:T(8,128)(2,1)}, bf16[2112,128]{1,0:T(8,128)(2,1)}) custom-call(s32[97]{0:T(128)} %get-tuple-element.55.rows, s32[97]{0:T(128)} %get-tuple-element.56.marks, bf16[1040,128]{1,0:T(8,128)(2,1)} %export_pages.1.refs_0_, bf16[1040,128]{1,0:T(8,128)(2,1)} %copy-done.4, bf16[1040,128]{1,0:T(8,128)(2,1)} %copy-done.6, ...), custom_call_target="tpu_custom_call" | custom-call | tf_op jit(solution)/shard_map/pack/pallas_call | solution.py:132
  51.0 1.7 %collective-permute-start.17 = (bf16[2112,128]{1,0:T(8,128)(2,1)}, bf16[2112,128]{1,0:T(8,128)(2,1)}, u32[]{:S(2)}, u32[]{:S(2)}) collective-permute-start(bf16[2112,128]{1,0:T(8,128)(2,1)} %get-tuple-element.61), channel_id=1, source_target_pairs={{0,8},{8,16},{16,24},{24,0},{32,40},{40,48},{48,56},{56,32},{64,72... | collective-permute-start | bytes 1622024 | tf_op jit(solution)/shard_map/key_side/ppermute | solution.py:47
  53.2 2.1 %collective-permute-start.16 = (bf16[2112,128]{1,0:T(8,128)(2,1)}, bf16[2112,128]{1,0:T(8,128)(2,1)}, u32[]{:S(2)}, u32[]{:S(2)}) collective-permute-start(bf16[2112,128]{1,0:T(8,128)(2,1)} %get-tuple-element.62), channel_id=1, source_target_pairs={{0,16},{8,24},{16,0},{24,8},{32,48},{40,56},{48,32},{56,40},{64,80... | collective-permute-start | bytes 1622024 | tf_op jit(solution)/shard_map/key_side/ppermute | solution.py:47
  55.3 1.4 %collective-permute-start.15 = (bf16[2112,128]{1,0:T(8,128)(2,1)}, bf16[2112,128]{1,0:T(8,128)(2,1)}, u32[]{:S(2)}, u32[]{:S(2)}) collective-permute-start(bf16[2112,128]{1,0:T(8,128)(2,1)} %get-tuple-element.63), channel_id=1, source_target_pairs={{0,24},{8,0},{16,8},{24,16},{32,56},{40,32},{48,40},{56,48},{64,88... | collective-permute-start | bytes 1622024 | tf_op jit(solution)/shard_map/key_side/ppermute | solution.py:47
  58.4 3.3 %pack.3 = (bf16[2048,128]{1,0:T(8,128)(2,1)}, bf16[2048,128]{1,0:T(8,128)(2,1)}, bf16[2048,128]{1,0:T(8,128)(2,1)}) custom-call(s32[97]{0:T(128)} %get-tuple-element.55.rows, s32[97]{0:T(128)} %get-tuple-element.56.marks, bf16[1040,128]{1,0:T(8,128)(2,1)} %export_pages.1.refs_0_, bf16[1040,128]{1,0:T(8,128)(2,1)} %copy-done.4, bf16[1040,128]{1,0:T(8,128)(2,1)} %copy-done.6, ...), custom_call_target="tpu_custom_call" | custom-call | tf_op jit(solution)/shard_map/pack/pallas_call | solution.py:132
  61.8 2.2 %copy-done.16 = bf16[4096,512]{1,0:T(8,128)(2,1)S(1)} copy-done((bf16[4096,512]{1,0:T(8,128)(2,1)S(1)}, bf16[4096,512]{1,0:T(8,128)(2,1)}, u32[]{:S(2)}) %copy-start.16) | copy-done | bytes 4194328
  64.0 1.6 %copy-done.17 = bf16[2,4096,128]{2,1,0:T(8,128)(2,1)S(1)} copy-done((bf16[2,4096,128]{2,1,0:T(8,128)(2,1)S(1)}, bf16[2,4096,128]{2,1,0:T(8,128)(2,1)}, u32[]{:S(2)}) %copy-start.17) | copy-done | bytes 2097176
  67.7 6.5 %project.1 = (bf16[2048,128]{1,0:T(8,128)(2,1)S(1)}, bf16[512,128]{1,0:T(8,128)(2,1)S(1)}, bf16[512,128]{1,0:T(8,128)(2,1)S(1)}) custom-call(s32[2]{0:T(128)S(1)} %pad_add_fusion.place, bf16[512,512]{1,0:T(8,128)(2,1)S(1)} %reshape.50.refs_0_, bf16[512,512]{1,0:T(8,128)(2,1)} %collective-permute-done.7.refs_1_, ...), custom_call_target="tpu_custom_call" | custom-call | tf_op jit(solution)/shard_map/project/pallas_call | solution.py:186
  75.7 2.1 %collective-permute-start.18 = (bf16[2048,128]{1,0:T(8,128)(2,1)}, bf16[2048,128]{1,0:T(8,128)(2,1)S(1)}, u32[]{:S(2)}, u32[]{:S(2)}) collective-permute-start(bf16[2048,128]{1,0:T(8,128)(2,1)} %get-tuple-element.72), channel_id=1, source_target_pairs={{0,24},{8,0},{16,8},{24,16},{32,56},{40,32},{48,40},{56,48},{64,88... | collective-permute-start | bytes 1572872 | tf_op jit(solution)/shard_map/value_side/ppermute | solution.py:47
  79.3 2.5 %collective-permute-done.15.refs_8_ = bf16[2112,128]{1,0:T(8,128)(2,1)} collective-permute-done((bf16[2112,128]{1,0:T(8,128)(2,1)}, bf16[2112,128]{1,0:T(8,128)(2,1)}, u32[]{:S(2)}, u32[]{:S(2)}) %collective-permute-start.15) | collective-permute-done | bytes 540704 | tf_op jit(solution)/shard_map/key_side/ppermute | solution.py:47
  83.1 10.9 %score.1 = (bf16[2048,512]{1,0:T(8,128)(2,1)S(1)}, f32[2048,128]{1,0:T(8,128)S(1)}) custom-call(s32[1024]{0:T(1024)S(1)} %reshape.47.table, s32[96]{0:T(128)S(1)} %copy-done.26, s32[96]{0:T(128)S(1)} %copy-done.27, s32[128]{0:T(128)S(1)} %copy-done.24, bf16[2048,128]{1,0:T(8,128)(2,1)S(1)} %copy-done.23, bf16[512,128]{1,0:T(8,128)(2,1)S(1)} %get-tuple-element.67.k_new, ...), custom_call_target="tpu_custom_call" | custom-call | tf_op jit(solution)/shard_map/score/pallas_call | solution.py:307
  94.0 9.1 %collective-permute-done.18.refs_8_ = bf16[2048,128]{1,0:T(8,128)(2,1)S(1)} collective-permute-done((bf16[2048,128]{1,0:T(8,128)(2,1)}, bf16[2048,128]{1,0:T(8,128)(2,1)S(1)}, u32[]{:S(2)}, u32[]{:S(2)}) %collective-permute-start.18) | collective-permute-done | bytes 524320 | tf_op jit(solution)/shard_map/value_side/ppermute | solution.py:47
  103.2 5.3 %value.1.near = bf16[512,512]{1,0:T(8,128)(2,1)S(1)} custom-call(s32[1024]{0:T(1024)S(1)} %reshape.47.table, s32[96]{0:T(128)S(1)} %copy-done.25, bf16[2048,512]{1,0:T(8,128)(2,1)S(1)} %get-tuple-element.69.weights, f32[2048,128]{1,0:T(8,128)S(1)} %get-tuple-element.70.fresh, bf16[1040,128]{1,0:T(8,128)(2,1)S(1)} %copy-done.1, ...), custom_call_target="tpu_custom_call" | custom-call | tf_op jit(solution)/shard_map/value/pallas_call | solution.py:354
  108.6 1.9 %collective-permute-done.21.far = bf16[512,512]{1,0:T(8,128)(2,1)S(1)} collective-permute-done((bf16[512,512]{1,0:T(8,128)(2,1)S(1)}, bf16[512,512]{1,0:T(8,128)(2,1)S(1)}, u32[]{:S(2)}, u32[]{:S(2)}) %collective-permute-start.21) | collective-permute-done | bytes 524320 | tf_op jit(solution)/shard_map/attended_core/ppermute | solution.py:58
  110.5 2.9 %mix.2 = (bf16[256,512]{1,0:T(8,128)(2,1)S(1)}, bf16[256,512]{1,0:T(8,128)(2,1)S(1)}) custom-call(s32[2]{0:T(128)S(1)} %pad_add_fusion.place, bf16[512,512]{1,0:T(8,128)(2,1)S(1)} %value.1.near, bf16[512,512]{1,0:T(8,128)(2,1)S(1)} %collective-permute-done.21.far, bf16[512,4096]{1,0:T(8,128)(2,1)S(1)} %copy-done, bf16[512,4096]{1,0:T(8,128)(2,1)} %collective-permute-done.1.w_far), custom_call_target="tpu_custom_call" | custom-call | tf_op jit(solution)/shard_map/mix/pallas_call | solution.py:389
  113.4 2.0 %collective-permute-start.26 = (bf16[256,512]{1,0:T(8,128)(2,1)S(1)}, bf16[256,512]{1,0:T(8,128)(2,1)S(1)}, u32[]{:S(2)}, u32[]{:S(2)}) collective-permute-start(bf16[256,512]{1,0:T(8,128)(2,1)S(1)} %get-tuple-element.84), channel_id=1, source_target_pairs={{0,6},{1,7},{2,0},{3,1},{4,2},{5,3},{6,4},{7,5},{8,14},{9,15},{10,... | collective-permute-start | bytes 786440 | tf_op jit(solution)/shard_map/output_relay/ppermute | solution.py:53
  115.7 4.0 %mix.3 = (bf16[256,512]{1,0:T(8,128)(2,1)S(1)}, bf16[256,512]{1,0:T(8,128)(2,1)S(1)}, bf16[256,512]{1,0:T(8,128)(2,1)S(1)}, bf16[256,512]{1,0:T(8,128)(2,1)S(1)}...) custom-call(s32[2]{0:T(128)S(1)} %pad_add_fusion.place, bf16[512,512]{1,0:T(8,128)(2,1)S(1)} %value.1.near, ...), custom_call_target="tpu_custom_call" | custom-call | tf_op jit(solution)/shard_map/mix/pallas_call | solution.py:389
  120.1 2.0 %collective-permute-done.26 = bf16[256,512]{1,0:T(8,128)(2,1)S(1)} collective-permute-done((bf16[256,512]{1,0:T(8,128)(2,1)S(1)}, bf16[256,512]{1,0:T(8,128)(2,1)S(1)}, u32[]{:S(2)}, u32[]{:S(2)}) %collective-permute-start.26) | collective-permute-done | bytes 262176 | tf_op jit(solution)/shard_map/output_relay/ppermute | solution.py:53
  122.1 3.0 %collective-permute-start.27 = (bf16[256,512]{1,0:T(8,128)(2,1)S(1)}, bf16[256,512]{1,0:T(8,128)(2,1)S(1)}, u32[]{:S(2)}, u32[]{:S(2)}) collective-permute-start(bf16[256,512]{1,0:T(8,128)(2,1)S(1)} %add_convert_fusion.1), channel_id=1, source_target_pairs={{0,6},{1,7},{2,0},{3,1},{4,2},{5,3},{6,4},{7,5},{8,14},{9,15},{10,... | collective-permute-start | bytes 786440 | tf_op jit(solution)/shard_map/output_far/ppermute | solution.py:53
  127.3 4.1 %collective-permute-done.25 = bf16[256,512]{1,0:T(8,128)(2,1)S(1)} collective-permute-done((bf16[256,512]{1,0:T(8,128)(2,1)S(1)}, bf16[256,512]{1,0:T(8,128)(2,1)S(1)}, u32[]{:S(2)}, u32[]{:S(2)}) %collective-permute-start.25) | collective-permute-done | bytes 262176 | tf_op jit(solution)/shard_map/output_near/ppermute | solution.py:53
  132.0 3.7 %collective-permute-done.22 = bf16[256,512]{1,0:T(8,128)(2,1)S(1)} collective-permute-done((bf16[256,512]{1,0:T(8,128)(2,1)S(1)}, bf16[256,512]{1,0:T(8,128)(2,1)S(1)}, u32[]{:S(2)}, u32[]{:S(2)}) %collective-permute-start.22) | collective-permute-done | bytes 262176 | tf_op jit(solution)/shard_map/output_near/ppermute | solution.py:53
  (119 shorter events, 22.5 us)
Async XLA Ops:
  0.0 40.4 %copy-start.28 = (s32[32,64]{1,0:T(8,128)S(1)}, s32[32,64]{1,0:T(8,128)}, u32[]{:S(2)}) copy-start(s32[32,64]{1,0:T(8,128)} %param.19) | copy-start | bytes 24580
  0.0 56.8 %copy-start.29 = (f32[4096]{0:T(1024)S(1)}, f32[4096]{0:T(1024)}, u32[]{:S(2)}) copy-start(f32[4096]{0:T(1024)} %param.12) | copy-start | bytes 49156
  0.0 16.5 %collective-permute-start.1 = (bf16[512,4096]{1,0:T(8,128)(2,1)}, bf16[512,4096]{1,0:T(8,128)(2,1)}, u32[]{:S(2)}, u32[]{:S(2)}) collective-permute-start(bf16[512,4096]{1,0:T(8,128)(2,1)} %w_near.3), channel_id=1, source_target_pairs={{0,1},{1,0},{2,3},{3,2},{4,5},{5,4},{6,7},{7,6},{8,9},{9,8},{10,11... | collective-permute-start | bytes 12582920 | tf_op jit(solution)/shard_map/w_out/ppermute | solution.py:58
  2.6 13.1 %collective-permute-start.3 = (bf16[1040,128]{1,0:T(8,128)(2,1)}, bf16[1040,128]{1,0:T(8,128)(2,1)S(1)}, u32[]{:S(2)}, u32[]{:S(2)}) collective-permute-start(bf16[1040,128]{1,0:T(8,128)(2,1)} %export_pages.1.refs_0_), channel_id=1, source_target_pairs={{0,32},{8,40},{16,48},{24,56},{32,64},{40,72},{48,80},{56,88},{64,... | collective-permute-start | bytes 798728 | tf_op jit(solution)/shard_map/pages1/ppermute | solution.py:41
  4.6 11.1 %collective-permute-start = (bf16[1040,128]{1,0:T(8,128)(2,1)}, bf16[1040,128]{1,0:T(8,128)(2,1)S(1)}, u32[]{:S(2)}, u32[]{:S(2)}) collective-permute-start(bf16[1040,128]{1,0:T(8,128)(2,1)} %export_pages.1.refs_0_), channel_id=1, source_target_pairs={{0,224},{8,232},{16,240},{24,248},{32,0},{40,8},{48,16},{56,24},{6... | collective-permute-start | bytes 798728 | tf_op jit(solution)/shard_map/pages1/ppermute | solution.py:41
  9.8 19.0 %collective-permute-start.8 = (bf16[512,512]{1,0:T(8,128)(2,1)S(1)}, bf16[512,512]{1,0:T(8,128)(2,1)}, u32[]{:S(2)}, u32[]{:S(2)}) collective-permute-start(bf16[512,512]{1,0:T(8,128)(2,1)S(1)} %reshape.50.refs_0_), channel_id=1, source_target_pairs={{0,4},{1,5},{2,6},{3,7},{4,0},{5,1},{6,2},{7,3},{8,12},{9,13},{10,... | collective-permute-start | bytes 1572872 | tf_op jit(solution)/shard_map/hidden/ppermute | solution.py:53
  13.1 23.9 %collective-permute-start.7 = (bf16[512,512]{1,0:T(8,128)(2,1)S(1)}, bf16[512,512]{1,0:T(8,128)(2,1)}, u32[]{:S(2)}, u32[]{:S(2)}) collective-permute-start(bf16[512,512]{1,0:T(8,128)(2,1)S(1)} %reshape.50.refs_0_), channel_id=1, source_target_pairs={{0,6},{1,7},{2,0},{3,1},{4,2},{5,3},{6,4},{7,5},{8,14},{9,15},{10,... | collective-permute-start | bytes 1572872 | tf_op jit(solution)/shard_map/hidden/ppermute | solution.py:53
  15.6 31.2 %copy-start.2 = (bf16[1040,128]{1,0:T(8,128)(2,1)}, bf16[1040,128]{1,0:T(8,128)(2,1)S(1)}, u32[]{:S(2)}) copy-start(bf16[1040,128]{1,0:T(8,128)(2,1)S(1)} %collective-permute-done.3.refs_7_) | copy-start | bytes 798724
  15.6 31.2 %copy-start.4 = (bf16[1040,128]{1,0:T(8,128)(2,1)}, bf16[1040,128]{1,0:T(8,128)(2,1)S(1)}, u32[]{:S(2)}) copy-start(bf16[1040,128]{1,0:T(8,128)(2,1)S(1)} %collective-permute-done.refs_1_) | copy-start | bytes 798724
  16.5 8.6 %collective-permute-start.2 = (bf16[1040,128]{1,0:T(8,128)(2,1)S(1)}, bf16[1040,128]{1,0:T(8,128)(2,1)S(1)}, u32[]{:S(2)}, u32[]{:S(2)}) collective-permute-start(bf16[1040,128]{1,0:T(8,128)(2,1)S(1)} %collective-permute-done.refs_1_), channel_id=1, source_target_pairs={{0,224},{8,232},{16,240},{24,248},{32,0},{40,8},{48,16},{56,24},{6... | collective-permute-start | bytes 798728 | tf_op jit(solution)/shard_map/pages2/ppermute | solution.py:41
  19.6 9.2 %collective-permute-start.5 = (bf16[1040,128]{1,0:T(8,128)(2,1)S(1)}, bf16[1040,128]{1,0:T(8,128)(2,1)S(1)}, u32[]{:S(2)}, u32[]{:S(2)}) collective-permute-start(bf16[1040,128]{1,0:T(8,128)(2,1)S(1)} %collective-permute-done.3.refs_7_), channel_id=1, source_target_pairs={{0,32},{8,40},{16,48},{24,56},{32,64},{40,72},{48,80},{56,88},{64,... | collective-permute-start | bytes 798728 | tf_op jit(solution)/shard_map/pages2/ppermute | solution.py:41
  25.1 13.6 %collective-permute-start.4 = (bf16[1040,128]{1,0:T(8,128)(2,1)S(1)}, bf16[1040,128]{1,0:T(8,128)(2,1)S(1)}, u32[]{:S(2)}, u32[]{:S(2)}) collective-permute-start(bf16[1040,128]{1,0:T(8,128)(2,1)S(1)} %collective-permute-done.2.refs_2_), channel_id=1, source_target_pairs={{0,224},{8,232},{16,240},{24,248},{32,0},{40,8},{48,16},{56,24},{6... | collective-permute-start | bytes 798728 | tf_op jit(solution)/shard_map/pages3/ppermute | solution.py:41
  28.8 9.9 %collective-permute-start.6 = (bf16[1040,128]{1,0:T(8,128)(2,1)S(1)}, bf16[1040,128]{1,0:T(8,128)(2,1)S(1)}, u32[]{:S(2)}, u32[]{:S(2)}) collective-permute-start(bf16[1040,128]{1,0:T(8,128)(2,1)S(1)} %collective-permute-done.5.refs_6_), channel_id=1, source_target_pairs={{0,32},{8,40},{16,48},{24,56},{32,64},{40,72},{48,80},{56,88},{64,... | collective-permute-start | bytes 798728 | tf_op jit(solution)/shard_map/pages3/ppermute | solution.py:41
  37.0 8.8 %collective-permute-start.10 = (bf16[512,512]{1,0:T(8,128)(2,1)}, bf16[512,512]{1,0:T(8,128)(2,1)}, u32[]{:S(2)}, u32[]{:S(2)}) collective-permute-start(bf16[512,512]{1,0:T(8,128)(2,1)} %collective-permute-done.7.refs_1_), channel_id=1, source_target_pairs={{0,1},{1,0},{2,3},{3,2},{4,5},{5,4},{6,7},{7,6},{8,9},{9,8},{10,11... | collective-permute-start | bytes 1572872 | tf_op jit(solution)/shard_map/hidden_core/ppermute | solution.py:58
  37.0 8.8 %collective-permute-start.11 = (bf16[512,512]{1,0:T(8,128)(2,1)}, bf16[512,512]{1,0:T(8,128)(2,1)}, u32[]{:S(2)}, u32[]{:S(2)}) collective-permute-start(bf16[512,512]{1,0:T(8,128)(2,1)} %collective-permute-done.8.refs_2_), channel_id=1, source_target_pairs={{0,1},{1,0},{2,3},{3,2},{4,5},{5,4},{6,7},{7,6},{8,9},{9,8},{10,11... | collective-permute-start | bytes 1572872 | tf_op jit(solution)/shard_map/hidden_core/ppermute | solution.py:58
  37.5 15.2 %collective-permute-start.9 = (bf16[512,512]{1,0:T(8,128)(2,1)S(1)}, bf16[512,512]{1,0:T(8,128)(2,1)}, u32[]{:S(2)}, u32[]{:S(2)}) collective-permute-start(bf16[512,512]{1,0:T(8,128)(2,1)S(1)} %reshape.50.refs_0_), channel_id=1, source_target_pairs={{0,2},{1,3},{2,4},{3,5},{4,6},{5,7},{6,0},{7,1},{8,10},{9,11},{10,... | collective-permute-start | bytes 1572872 | tf_op jit(solution)/shard_map/hidden/ppermute | solution.py:53
  38.7 8.1 %collective-permute-start.12 = (bf16[1040,128]{1,0:T(8,128)(2,1)S(1)}, bf16[1040,128]{1,0:T(8,128)(2,1)S(1)}, u32[]{:S(2)}, u32[]{:S(2)}) collective-permute-start(bf16[1040,128]{1,0:T(8,128)(2,1)S(1)} %collective-permute-done.4.refs_3_), channel_id=1, source_target_pairs={{0,224},{8,232},{16,240},{24,248},{32,0},{40,8},{48,16},{56,24},{6... | collective-permute-start | bytes 798728 | tf_op jit(solution)/shard_map/pages4/ppermute | solution.py:41
  51.0 26.8 %collective-permute-start.17 = (bf16[2112,128]{1,0:T(8,128)(2,1)}, bf16[2112,128]{1,0:T(8,128)(2,1)}, u32[]{:S(2)}, u32[]{:S(2)}) collective-permute-start(bf16[2112,128]{1,0:T(8,128)(2,1)} %get-tuple-element.61), channel_id=1, source_target_pairs={{0,8},{8,16},{16,24},{24,0},{32,40},{40,48},{48,56},{56,32},{64,72... | collective-permute-start | bytes 1622024 | tf_op jit(solution)/shard_map/key_side/ppermute | solution.py:47
  52.7 4.1 %collective-permute-start.13 = (bf16[512,512]{1,0:T(8,128)(2,1)S(1)}, bf16[512,512]{1,0:T(8,128)(2,1)S(1)}, u32[]{:S(2)}, u32[]{:S(2)}) collective-permute-start(bf16[512,512]{1,0:T(8,128)(2,1)S(1)} %reshape.50.refs_0_), channel_id=1, source_target_pairs={{0,1},{1,0},{2,3},{3,2},{4,5},{5,4},{6,7},{7,6},{8,9},{9,8},{10,11... | collective-permute-start | bytes 1572872 | tf_op jit(solution)/shard_map/hidden_core/ppermute | solution.py:58
  52.7 4.9 %collective-permute-start.14 = (bf16[512,512]{1,0:T(8,128)(2,1)}, bf16[512,512]{1,0:T(8,128)(2,1)S(1)}, u32[]{:S(2)}, u32[]{:S(2)}) collective-permute-start(bf16[512,512]{1,0:T(8,128)(2,1)} %collective-permute-done.9.refs_3_), channel_id=1, source_target_pairs={{0,1},{1,0},{2,3},{3,2},{4,5},{5,4},{6,7},{7,6},{8,9},{9,8},{10,11... | collective-permute-start | bytes 1572872 | tf_op jit(solution)/shard_map/hidden_core/ppermute | solution.py:58
  53.2 26.1 %collective-permute-start.16 = (bf16[2112,128]{1,0:T(8,128)(2,1)}, bf16[2112,128]{1,0:T(8,128)(2,1)}, u32[]{:S(2)}, u32[]{:S(2)}) collective-permute-start(bf16[2112,128]{1,0:T(8,128)(2,1)} %get-tuple-element.62), channel_id=1, source_target_pairs={{0,16},{8,24},{16,0},{24,8},{32,48},{40,56},{48,32},{56,40},{64,80... | collective-permute-start | bytes 1622024 | tf_op jit(solution)/shard_map/key_side/ppermute | solution.py:47
  55.3 26.6 %collective-permute-start.15 = (bf16[2112,128]{1,0:T(8,128)(2,1)}, bf16[2112,128]{1,0:T(8,128)(2,1)}, u32[]{:S(2)}, u32[]{:S(2)}) collective-permute-start(bf16[2112,128]{1,0:T(8,128)(2,1)} %get-tuple-element.63), channel_id=1, source_target_pairs={{0,24},{8,0},{16,8},{24,16},{32,56},{40,32},{48,40},{56,48},{64,88... | collective-permute-start | bytes 1622024 | tf_op jit(solution)/shard_map/key_side/ppermute | solution.py:47
  75.1 19.0 %collective-permute-start.19 = (bf16[2048,128]{1,0:T(8,128)(2,1)}, bf16[2048,128]{1,0:T(8,128)(2,1)S(1)}, u32[]{:S(2)}, u32[]{:S(2)}) collective-permute-start(bf16[2048,128]{1,0:T(8,128)(2,1)} %get-tuple-element.74), channel_id=1, source_target_pairs={{0,16},{8,24},{16,0},{24,8},{32,48},{40,56},{48,32},{56,40},{64,80... | collective-permute-start | bytes 1572872 | tf_op jit(solution)/shard_map/value_side/ppermute | solution.py:47
  75.7 27.5 %collective-permute-start.18 = (bf16[2048,128]{1,0:T(8,128)(2,1)}, bf16[2048,128]{1,0:T(8,128)(2,1)S(1)}, u32[]{:S(2)}, u32[]{:S(2)}) collective-permute-start(bf16[2048,128]{1,0:T(8,128)(2,1)} %get-tuple-element.72), channel_id=1, source_target_pairs={{0,24},{8,0},{16,8},{24,16},{32,56},{40,32},{48,40},{56,48},{64,88... | collective-permute-start | bytes 1572872 | tf_op jit(solution)/shard_map/value_side/ppermute | solution.py:47
  77.7 25.4 %collective-permute-start.20 = (bf16[2048,128]{1,0:T(8,128)(2,1)}, bf16[2048,128]{1,0:T(8,128)(2,1)}, u32[]{:S(2)}, u32[]{:S(2)}) collective-permute-start(bf16[2048,128]{1,0:T(8,128)(2,1)} %get-tuple-element.75), channel_id=1, source_target_pairs={{0,8},{8,16},{16,24},{24,0},{32,40},{40,48},{48,56},{56,32},{64,72... | collective-permute-start | bytes 1572872 | tf_op jit(solution)/shard_map/value_side/ppermute | solution.py:47
  108.5 2.0 %collective-permute-start.21 = (bf16[512,512]{1,0:T(8,128)(2,1)S(1)}, bf16[512,512]{1,0:T(8,128)(2,1)S(1)}, u32[]{:S(2)}, u32[]{:S(2)}) collective-permute-start(bf16[512,512]{1,0:T(8,128)(2,1)S(1)} %value.1.near), channel_id=1, source_target_pairs={{0,1},{1,0},{2,3},{3,2},{4,5},{5,4},{6,7},{7,6},{8,9},{9,8},{10,11... | collective-permute-start | bytes 1572872 | tf_op jit(solution)/shard_map/attended_core/ppermute | solution.py:58
  113.4 8.6 %collective-permute-start.26 = (bf16[256,512]{1,0:T(8,128)(2,1)S(1)}, bf16[256,512]{1,0:T(8,128)(2,1)S(1)}, u32[]{:S(2)}, u32[]{:S(2)}) collective-permute-start(bf16[256,512]{1,0:T(8,128)(2,1)S(1)} %get-tuple-element.84), channel_id=1, source_target_pairs={{0,6},{1,7},{2,0},{3,1},{4,2},{5,3},{6,4},{7,5},{8,14},{9,15},{10,... | collective-permute-start | bytes 786440 | tf_op jit(solution)/shard_map/output_relay/ppermute | solution.py:53
  115.4 10.4 %collective-permute-start.23 = (bf16[256,512]{1,0:T(8,128)(2,1)S(1)}, bf16[256,512]{1,0:T(8,128)(2,1)S(1)}, u32[]{:S(2)}, u32[]{:S(2)}) collective-permute-start(bf16[256,512]{1,0:T(8,128)(2,1)S(1)} %get-tuple-element.76), channel_id=1, source_target_pairs={{0,2},{1,3},{2,4},{3,5},{4,6},{5,7},{6,0},{7,1},{8,10},{9,11},{10,... | collective-permute-start | bytes 786440 | tf_op jit(solution)/shard_map/output_relay/ppermute | solution.py:53
  119.7 11.7 %collective-permute-start.25 = (bf16[256,512]{1,0:T(8,128)(2,1)S(1)}, bf16[256,512]{1,0:T(8,128)(2,1)S(1)}, u32[]{:S(2)}, u32[]{:S(2)}) collective-permute-start(bf16[256,512]{1,0:T(8,128)(2,1)S(1)} %get-tuple-element.82), channel_id=1, source_target_pairs={{0,2},{1,3},{2,4},{3,5},{4,6},{5,7},{6,0},{7,1},{8,10},{9,11},{10,... | collective-permute-start | bytes 786440 | tf_op jit(solution)/shard_map/output_near/ppermute | solution.py:53
  122.1 9.8 %collective-permute-start.27 = (bf16[256,512]{1,0:T(8,128)(2,1)S(1)}, bf16[256,512]{1,0:T(8,128)(2,1)S(1)}, u32[]{:S(2)}, u32[]{:S(2)}) collective-permute-start(bf16[256,512]{1,0:T(8,128)(2,1)S(1)} %add_convert_fusion.1), channel_id=1, source_target_pairs={{0,6},{1,7},{2,0},{3,1},{4,2},{5,3},{6,4},{7,5},{8,14},{9,15},{10,... | collective-permute-start | bytes 786440 | tf_op jit(solution)/shard_map/output_far/ppermute | solution.py:53
  125.1 10.7 %collective-permute-start.22 = (bf16[256,512]{1,0:T(8,128)(2,1)S(1)}, bf16[256,512]{1,0:T(8,128)(2,1)S(1)}, u32[]{:S(2)}, u32[]{:S(2)}) collective-permute-start(bf16[256,512]{1,0:T(8,128)(2,1)S(1)} %get-tuple-element.79), channel_id=1, source_target_pairs={{0,6},{1,7},{2,0},{3,1},{4,2},{5,3},{6,4},{7,5},{8,14},{9,15},{10,... | collective-permute-start | bytes 786440 | tf_op jit(solution)/shard_map/output_near/ppermute | solution.py:53
  125.9 10.0 %collective-permute-start.24 = (bf16[256,512]{1,0:T(8,128)(2,1)S(1)}, bf16[256,512]{1,0:T(8,128)(2,1)S(1)}, u32[]{:S(2)}, u32[]{:S(2)}) collective-permute-start(bf16[256,512]{1,0:T(8,128)(2,1)S(1)} %add_convert_fusion.3), channel_id=1, source_target_pairs={{0,2},{1,3},{2,4},{3,5},{4,6},{5,7},{6,0},{7,1},{8,10},{9,11},{10,... | collective-permute-start | bytes 786440 | tf_op jit(solution)/shard_map/output_far/ppermute | solution.py:53
  (28 other events, 288.4 us)
